TPU v7x, 256 devices: a whole 4x4x8 slice. The times are simulated.
256 devices in a mesh: leaf: 8 (over z), row: 4 (over y), col: 8 (over x, core).
Axes of the slice: x: 4, y: 4, z: 8, core: 2. Of those that a mesh axis runs over, the one named last changes fastest.
Arguments:
- rhs_child: bfloat16 [8, 128, 6144], P('leaf', None, 'col'), may hold values from -6 to 6
- rhs_root: float32 [128, 12288], P(None, 'col'), may hold values from -6 to 6
- fwd_child: bfloat16 [8, 6144, 6144], P('leaf', 'col', 'row'), may hold values from -0.078125 to 0.078125
- coupling: bfloat16 [8, 6144, 4096], P('leaf', 'row', 'col'), may hold values from -0.078125 to 0.078125
- root_inverse: bfloat16 [12288, 12288], P('col', ('leaf', 'row')), may hold values from -0.0546875 to 0.0546875
- back_child: bfloat16 [8, 4096, 6144], P('leaf', None, ('row', 'col')), may hold values from -0.09375 to 0.09375
- bwd_child: bfloat16 [8, 6144, 6144], P('leaf', ('row', 'col')), may hold values from -0.078125 to 0.078125
- parent_rows: int32 [8, 4096], P('leaf'), may hold values from 0 to 12287, as said below
Outputs:
- x_root: float32 [128, 12288], P(None, ('leaf', 'row', 'col'))
- x_child: float32 [8, 128, 6144], P('leaf', None, ('row', 'col'))
Inputs may be any that keep to these rules, and one draw needn't show every extreme that they name: For each child, the entries parent_rows[c, q * 512 + i] for 0 <= i < 512 are distinct and lie in q * 1536 to (q + 1) * 1536 - 1.
All inputs are finite; a program needn't handle non-finite values.
Results may differ from a plain program's by a relative error of at most 0.009.
Values may be sent and summed in bfloat16 or wider, within the bound.
A program may use at most 64 MiB of HBM per device.

v0:
```python
import jax
import jax.numpy as jnp
from jax import lax
from jax.sharding import PartitionSpec as P


def product(left, right):
    return jnp.dot(
        left.astype(jnp.float32),
        right.astype(jnp.float32),
        precision=lax.Precision.HIGHEST,
        preferred_element_type=jnp.float32,
    )


def local(
    rhs_child, rhs_root, fwd_child, coupling, root_inverse, back_child, bwd_child, parent_rows
):
    col_pos = lax.axis_index("col")
    col_count = lax.axis_size("col")
    partial_y = product(rhs_child[0], fwd_child[0])
    child_y = lax.psum(partial_y, "col")
    partial_u = product(child_y.astype(jnp.bfloat16), coupling[0])
    part_width = coupling.shape[2]
    block_width = rhs_root.shape[1]
    local_rows = (
        lax.dynamic_slice_in_dim(parent_rows[0], col_pos * part_width, part_width)
        - col_pos * block_width
    )
    placing = (local_rows[:, None] == jnp.arange(block_width, dtype=jnp.int32)[None, :]).astype(
        jnp.float32
    )
    assembled = lax.psum(
        jnp.dot(
            partial_u, placing, precision=lax.Precision.HIGHEST, preferred_element_type=jnp.float32
        ),
        ("leaf", "row"),
    )
    parent_rhs = (rhs_root - assembled).astype(jnp.bfloat16)
    partial_x = product(parent_rhs, root_inverse)
    share_width = partial_x.shape[1] // col_count
    root_block = lax.psum(partial_x, "col")
    x_root = lax.dynamic_slice_in_dim(root_block, col_pos * share_width, share_width, 1)
    full_root = lax.all_gather(root_block.astype(jnp.bfloat16), ("leaf", "row"), axis=1, tiled=True)
    block_rows = (
        parent_rows[0].reshape(col_count, part_width)
        - (jnp.arange(col_count, dtype=jnp.int32) * block_width)[:, None]
    )
    picking = (
        block_rows[:, None, :] == jnp.arange(block_width, dtype=jnp.int32)[None, :, None]
    ).astype(jnp.float32)
    root_blocks = full_root.astype(jnp.float32).reshape(full_root.shape[0], col_count, block_width)
    selected = jnp.einsum(
        "kqp,qpi->kqi",
        root_blocks,
        picking,
        precision=lax.Precision.HIGHEST,
        preferred_element_type=jnp.float32,
    )
    selected = selected.reshape(full_root.shape[0], col_count * part_width)
    correction = product(selected, back_child[0])
    narrow = correction.shape[1]
    own_y = lax.dynamic_slice_in_dim(child_y, col_pos * narrow, narrow, 1)
    reduced = (own_y - correction).astype(jnp.bfloat16)
    partial_child = product(reduced, bwd_child[0])
    child_x = lax.psum_scatter(partial_child, ("row", "col"), scatter_dimension=1, tiled=True)
    return (x_root, child_x[None])


def solution(mesh):
    placed = (
        P("leaf", None, "col"),
        P(None, "col"),
        P("leaf", "col", "row"),
        P("leaf", "row", "col"),
        P("col", ("leaf", "row")),
        P("leaf", None, ("row", "col")),
        P("leaf", ("row", "col"), None),
        P("leaf", None),
    )
    return jax.shard_map(
        local,
        mesh=mesh,
        in_specs=placed,
        out_specs=(P(None, ("leaf", "row", "col")), P("leaf", None, ("row", "col"))),
        check_vma=False,
    )
```

profile of v0, /device:TPU:1, one launch (start us, length us, event | category | flops | bytes accessed | tf_op | source)
XLA Modules:
  0.0 484.4 jit_solution(14617228594558310990)
XLA Ops:
  7.2 0.0 copy-start
  7.2 0.0 copy-start.3
  7.2 0.0 all-reduce.4.cloned.1.call-start
  7.2 3.3 fusion.7
  10.5 0.0 all-reduce.4.cloned.1.call-update
  10.6 0.0 all-reduce.6.cloned.1.call-start
  10.6 0.0 copy-done.3
  10.6 0.6 dynamic-slice_subtract_fusion
  11.2 0.0 copy-start.2
  11.2 68.0 %all-reduce.4.cloned.1.call-done = f32[128,1536]{1,0:T(8,128)} async-done(((f32[128,1536]{1,0:T(8,128)}), f32[128,1536]{1,0:T(8,128)}) %all-reduce.4.cloned.1.call-update) | async-done | bytes 786448 | tf_op jit(solution)/shard_map/psum | solution.py:22
  79.2 0.0 copy-start.4
  79.2 2.0 fusion.11
  81.3 0.0 copy-done.4
  81.3 2.2 fusion.4
  83.4 0.0 all-reduce.6.cloned.1.call-update
  83.5 0.0 all-reduce.8.cloned.1.call-start
  83.5 145.4 %all-reduce.6.cloned.1.call-done = f32[128,1536]{1,0:T(8,128)} async-done(((f32[128,1536]{1,0:T(8,128)}), f32[128,1536]{1,0:T(8,128)}) %all-reduce.6.cloned.1.call-update) | async-done | bytes 786448 | tf_op jit(solution)/shard_map/psum | solution.py:33
  228.9 0.0 copy-done.2
  228.9 2.4 fusion.20
  231.3 0.0 all-reduce.8.cloned.1.call-update
  231.3 0.0 all-gather.2.cloned.1.call-start
  231.4 64.8 %all-reduce.8.cloned.1.call-done = f32[128,384]{1,0:T(8,128)} async-done(((f32[128,384]{1,0:T(8,128)}), f32[128,384]{1,0:T(8,128)}) %all-reduce.8.cloned.1.call-update) | async-done | bytes 196624 | tf_op jit(solution)/shard_map/psum | solution.py:42
  296.1 1.6 convert_element_type.10
  297.7 0.0 all-gather.2.cloned.1.call-update
  297.7 0.0 reduce-scatter.2.cloned.1.call-start
  297.8 0.5 broadcast.26
  298.3 0.7 reduce.3
  299.0 0.1 broadcast_subtract_fusion
  299.1 77.3 %all-gather.2.cloned.1.call-done = bf16[128,12288]{1,0:T(8,128)(2,1)} async-done(((bf16[128,384]{1,0:T(8,128)(2,1)}), bf16[128,12288]{1,0:T(8,128)(2,1)}) %all-gather.2.cloned.1.call-update) | async-done | bytes 3145744 | tf_op jit(solution)/shard_map/all_gather | solution.py:44
  376.4 0.0 copy-start.1
  376.4 6.1 %fusion = f32[8,512,128]{2,1,0:T(8,128)S(1)} fusion(s32[8,512]{1,0:T(8,128)S(1)} %broadcast_subtract_fusion, bf16[16,8,8,1536]{3,2,1,0:T(8,128)(2,1)} %bitcast.34), kind=kOutput, calls=%fused_computation.1 | convolution fusion | flops 1616904192 | bytes 5259264 | tf_op jit(solution)/shard_map/kqp,qpi->kqi/dot_general | solution.py:53
  382.6 0.0 copy-done.1
  382.6 2.8 fusion.17
  385.4 0.0 copy-done
  385.4 3.0 fusion.5
  388.4 0.0 reduce-scatter.2.cloned.1.call-update
  388.5 1.0 constant_dynamic-slice_fusion
  389.4 0.7 copy.11
  390.1 87.7 %reduce-scatter.2.cloned.1.call-done = f32[128,192]{0,1:T(8,128)} async-done(((f32[128,6144]{0,1:T(8,128)}), f32[128,192]{0,1:T(8,128)}) %reduce-scatter.2.cloned.1.call-update) | async-done | bytes 98320 | tf_op jit(solution)/shard_map/reduce_scatter | solution.py:66
  (2 shorter events, 0.0 us)
Async XLA Ops:
  7.2 378.3 %copy-start = (bf16[1,192,6144]{2,1,0:T(8,128)(2,1)S(1)}, bf16[1,192,6144]{2,1,0:T(8,128)(2,1)}, u32[]{:S(2)}) copy-start(bf16[1,192,6144]{2,1,0:T(8,128)(2,1)} %param.14) | copy-start | bytes 7077892
  7.2 3.4 copy-start.3
  7.2 72.0 %all-reduce.4.cloned.1.call-start = ((), (), s32[]{:S(2)}) async-start(), calls=%async_computation.1 | async-start | bytes 1572864 | tf_op jit(solution)/shard_map/psum | solution.py:22
  10.6 218.3 %all-reduce.6.cloned.1.call-start = ((), (), s32[]{:S(2)}) async-start(), calls=%async_computation.2 | async-start | bytes 1572864 | tf_op jit(solution)/shard_map/psum | solution.py:33
  11.2 217.7 %copy-start.2 = (bf16[1536,384]{1,0:T(8,128)(2,1)S(1)}, bf16[1536,384]{1,0:T(8,128)(2,1)}, u32[]{:S(2)}) copy-start(bf16[1536,384]{1,0:T(8,128)(2,1)} %param.12) | copy-start | bytes 3538948
  79.2 2.1 copy-start.4
  83.5 212.7 %all-reduce.8.cloned.1.call-start = ((), (), s32[]{:S(2)}) async-start(), calls=%async_computation.3 | async-start | bytes 393216 | tf_op jit(solution)/shard_map/psum | solution.py:42
  231.3 145.1 %all-gather.2.cloned.1.call-start = ((), (), s32[]{:S(2)}) async-start(), calls=%async_computation.4 | async-start | bytes 3244032 | tf_op jit(solution)/shard_map/all_gather | solution.py:44
  297.7 180.1 %reduce-scatter.2.cloned.1.call-start = ((), (), s32[]{:S(2)}) async-start(), calls=%async_computation.5 | async-start | bytes 3244032 | tf_op jit(solution)/shard_map/reduce_scatter | solution.py:66
  376.4 6.1 %copy-start.1 = (bf16[1,4096,192]{1,2,0:T(8,128)(2,1)S(1)}, bf16[1,4096,192]{1,2,0:T(8,128)(2,1)}, u32[]{:S(2)}) copy-start(bf16[1,4096,192]{1,2,0:T(8,128)(2,1)} %param.13) | copy-start | bytes 4718596
Sparse Core Ops, SparseCore 0:
  10.7 68.4 all-reduce.3
  83.6 145.2 all-reduce.5
  231.5 64.6 all-reduce.7
  299.1 77.2 all-gather.1
  388.6 89.2 reduce-scatter.1
where the time goes:
time: 485 us; the launch traced here: 484 us
  waiting for transfers between devices  443 us (91%)
  matrix products  21.9 us (5%)
  between operations  13.9 us (3%)
    psum x1, waiting for transfers between devices, local(): lax.psum(jnp.dot(partial_u, placing, precision=lax.Precision.HIGHEST, pre...  145 us
    reduce_scatter x1, waiting for transfers between devices, local(): lax.psum_scatter(partial_child, ('row', 'col'), scatter_dimension=1, tile...  87.7 us
    all_gather x1, waiting for transfers between devices, local(): lax.all_gather(root_block.astype(jnp.bfloat16), ('leaf', 'row'), axis=1,...  77.3 us
    psum x1, waiting for transfers between devices, local(): child_y = lax.psum(partial_y, 'col')  68 us
    psum x1, waiting for transfers between devices, local(): root_block = lax.psum(partial_x, 'col')  64.8 us
    dot_general x5, matrix products, product(): jnp.dot(left.astype(jnp.float32), right.astype(jnp.float32), precision=la...  13.6 us
  transfers between devices with their start and end apart: 5, of which 5 were waited for; matrix products, arithmetic and copies ran while one was open for 1% of the time, Pallas kernels for 0%

commit v1 on v0

v1 whole, which is shorter than its diff:
```python
import jax
import jax.numpy as jnp
from jax import lax
from jax.experimental import pallas as pl
from jax.experimental.pallas import tpu as pltpu
from jax.sharding import PartitionSpec as P

BF = jnp.bfloat16
F32 = jnp.float32
MESH = pl.DeviceIdType.MESH
CONTRACT_LAST = (((1,), (1,)), ((), ()))

X_ORDER = (2, 1, 3)
Y_ORDER = (2, 1, 3)
Z_ORDER = (4, 3, 5, 2, 6, 1, 7)
Z_ARRIVAL = (1, 7, 2, 6, 3, 5, 4)
PLANE = sorted(
    ((dy, dx) for dy in range(4) for dx in range(4) if (dy, dx) != (0, 0)),
    key=lambda p: -(min(p[0], 4 - p[0]) + min(p[1], 4 - p[1])),
)
COL = [(dx, dh) for dx in (2, 1, 3) for dh in (1, 0)] + [(0, 1)]


def dot(a, b):
    return jnp.dot(a, b, preferred_element_type=F32)


def dot_last(a, b):
    return lax.dot_general(a, b, CONTRACT_LAST, preferred_element_type=F32)


def kernel(
    rhs_ref, root_ref, fwd_ref, coup_ref, rinv_ref, back_ref, bwd_ref, rows_ref,
    xroot_ref, xchild_ref,
    rhs_v, fwd_v, coup_v, rinv_v, back_v, bwd_v, root_v, rows_v,
    part_f, part_b, core_in, x_out, x_in, y_keep, y_all,
    u_f, u_b, u_in, u_all, place, pick, p_rhs,
    xp_f, xp_b, xp_in, xr_all, rb_all, sel_out, sel_in, sel_all,
    z_out, z_in, zsum, flip,
    load_sem, core_s, core_r, xs_s, xs_r, ag_s, ag_r, fw_s, fw_r,
    us_s, us_r, za_s, za_r, pr_s, pr_r, ya_s, ya_r, xc_s, xc_r, xo_s, xo_r,
    rb_s, rb_r, se_s, se_r, pl_s, pl_r, fin_s, fin_r, end_s, end_r, w_s, w_r,
):
    l, r, q = lax.axis_index("leaf"), lax.axis_index("row"), lax.axis_index("col")
    x, h = q // 2, q % 2
    sib = (l, r, x * 2 + 1 - h)

    def xat(d):
        return lax.rem(x + d, 4)

    def yat(d):
        return lax.rem(r + d, 4)

    def zat(d):
        return lax.rem(l + d, 8)

    def load(src, dst, k):
        c = pltpu.make_async_copy(src, dst, load_sem.at[k])
        c.start()
        return c

    pending = []

    def send(src, dst, ss, rs, device):
        c = pltpu.make_async_remote_copy(
            src_ref=src, dst_ref=dst, send_sem=ss, recv_sem=rs, device_id=device, device_id_type=MESH
        )
        c.start()
        pending.append(c)

    def arrive(dst, ss, rs):
        pltpu.make_async_remote_copy(
            src_ref=dst, dst_ref=dst, send_sem=ss, recv_sem=rs, device_id=sib, device_id_type=MESH
        ).wait_recv()

    def flush():
        while pending:
            pending.pop(0).wait_send()

    partners = [(l, r, xat(dx) * 2 + lax.rem(h + dh, 2)) for dx, dh in COL]
    partners += [(l, yat(dy), xat(dx) * 2 + h) for dy, dx in PLANE if dy]
    partners += [(zat(d), r, q) for d in Z_ORDER]
    bar = pltpu.get_barrier_semaphore()
    for p in partners:
        pl.semaphore_signal(bar, inc=1, device_id=p, device_id_type=MESH)

    l_rhs = load(rhs_ref, rhs_v, 0)
    l_fwd = []
    for j, d in enumerate(X_ORDER + (0,)):
        cols = pl.ds(pl.multiple_of(xat(d) * 384, 128), 384)
        l_fwd.append(load(fwd_ref.at[:, cols], fwd_v.at[j], 1 + j))
    l_rows = load(rows_ref, rows_v.at[l], 5)
    l_coup = load(coup_ref, coup_v, 6)
    l_root = load(root_ref.at[pl.ds(pl.multiple_of(r * 32, 32), 32)], root_v, 7)
    l_rinv = load(rinv_ref, rinv_v, 8)
    l_back = load(back_ref, back_v.at[h], 9)
    l_bwd = load(bwd_ref, bwd_v.at[h], 10)

    mine = pl.ds(pl.multiple_of(h * 64, 64), 64)
    other = pl.ds(pl.multiple_of((1 - h) * 64, 64), 64)
    l_rhs.wait()
    for j in range(4):
        l_fwd[j].wait()
        value = dot(rhs_v[...], fwd_v[j])
        part_f[j] = value
        part_b[j] = value.astype(BF)
        if j == 0:
            pl.semaphore_wait(bar, len(partners))
        send(part_b.at[j, other], core_in.at[j], core_s.at[j], core_r.at[j], sib)
    for j, d in enumerate(X_ORDER + (0,)):
        arrive(core_in.at[j], core_s.at[j], core_r.at[j])
        both = part_f[j, mine, :] + core_in[j].astype(F32)
        if d:
            x_out[j] = both.astype(BF)
            send(x_out.at[j], x_in.at[j], xs_s.at[j], xs_r.at[j], (l, r, xat(d) * 2 + h))
        else:
            y_keep[...] = both

    l_rows.wait()
    for j, d in enumerate(Z_ORDER):
        send(rows_ref, rows_v.at[l], pr_s.at[j], pr_r.at[j], (zat(d), r, q))

    def build_place(leaf):
        row = rows_v[leaf, :, pl.ds(pl.multiple_of(q * 512, 512), 512)] - q * 1536

        @pl.loop(0, 12)
        def _(t):
            at = lax.broadcasted_iota(jnp.int32, (128, 512), 0) + t * 128
            place[leaf, pl.ds(pl.multiple_of(t * 128, 128), 128), :] = (at == row).astype(F32).astype(BF)

    def build_pick(leaf):
        row = rows_v[leaf, :, pl.ds(pl.multiple_of(l * 512 + r * 128, 128), 128)] - l * 1536

        @pl.loop(0, 12)
        def _(t):
            at = lax.broadcasted_iota(jnp.int32, (128, 128), 0) + t * 128
            pick[leaf, pl.ds(pl.multiple_of(t * 128, 128), 128), :] = (at == row).astype(F32).astype(BF)

    def rows_arrive(d):
        j = Z_ORDER.index((8 - d) % 8)
        arrive(rows_v.at[zat(d)], pr_s.at[j], pr_r.at[j])

    build_place(l)
    build_pick(l)
    for d in Z_ARRIVAL[:3]:
        rows_arrive(d)
        build_place(zat(d))
        build_pick(zat(d))

    total = y_keep[...]
    for j in range(3):
        arrive(x_in.at[j], xs_s.at[j], xs_r.at[j])
        total = total + x_in[j].astype(F32)
    y_keep[...] = total
    y_all[x, mine, :] = total.astype(BF)
    for j, d in enumerate(X_ORDER):
        send(y_all.at[x, mine], y_all.at[x, mine], ag_s.at[j], ag_r.at[j], (l, r, xat(d) * 2 + h))
    send(y_all.at[x, mine], y_all.at[x, mine], fw_s.at[3], fw_r.at[3], sib)
    for d in Z_ARRIVAL[3:]:
        rows_arrive(d)
        build_place(zat(d))
        build_pick(zat(d))
    l_coup.wait()
    for d in (1, 3, 2):
        j = X_ORDER.index((4 - d) % 4)
        src = xat(d)
        arrive(y_all.at[src, mine], ag_s.at[j], ag_r.at[j])
        send(y_all.at[src, mine], y_all.at[src, mine], fw_s.at[j], fw_r.at[j], sib)
    update = jnp.zeros((128, 512), F32)
    for d in (0, 1, 3, 2):
        j = X_ORDER.index((4 - d) % 4) if d else 3
        src = xat(d)
        arrive(y_all.at[src, other], fw_s.at[j], fw_r.at[j])
        update = update + dot(y_all[src], coup_v[pl.ds(pl.multiple_of(src * 384, 128), 384), :])

    u_f[...] = update
    u_b[...] = update.astype(BF)
    for j, d in enumerate(Y_ORDER):
        k = pl.ds(pl.multiple_of(yat(d) * 32, 32), 32)
        send(u_b.at[k], u_in.at[j], us_s.at[j], us_r.at[j], (l, yat(d), q))
    flush_before = list(pending)
    pending.clear()
    for c in flush_before[:-3]:
        c.wait_send()
    pending.extend(flush_before[-3:])
    l_back.wait()
    l_bwd.wait()
    send(back_v.at[h], back_v.at[h], w_s.at[0], w_r.at[0], sib)
    send(bwd_v.at[h], bwd_v.at[h], w_s.at[1], w_r.at[1], sib)
    my_k = pl.ds(pl.multiple_of(r * 32, 32), 32)
    total = u_f[my_k, :]
    for j in range(3):
        arrive(u_in.at[j], us_s.at[j], us_r.at[j])
        total = total + u_in[j].astype(F32)
    u_all[l] = total.astype(BF)

    for j, d in enumerate(Z_ORDER):
        send(u_all.at[l], u_all.at[l], za_s.at[j], za_r.at[j], (zat(d), r, q))
    l_root.wait()
    placed = dot_last(u_all[l], place[l])
    for d in Z_ARRIVAL:
        j = Z_ORDER.index((8 - d) % 8)
        leaf = zat(d)
        arrive(u_all.at[leaf], za_s.at[j], za_r.at[j])
        placed = placed + dot_last(u_all[leaf], place[leaf])
    p_rhs[my_k, :] = (root_v[...] - placed).astype(BF)

    for j, d in enumerate(Y_ORDER):
        send(p_rhs.at[my_k], p_rhs.at[my_k], ya_s.at[j], ya_r.at[j], (l, yat(d), q))
    l_rinv.wait()
    for j, d in enumerate(Y_ORDER):
        k = pl.ds(pl.multiple_of(yat(4 - d) * 32, 32), 32)
        arrive(p_rhs.at[k], ya_s.at[j], ya_r.at[j])
    value = dot(p_rhs[...], rinv_v[...])

    xp_f[...] = value
    xp_b[...] = value.astype(BF)
    for j, (dx, dh) in enumerate(COL):
        tx, th = xat(dx), lax.rem(h + dh, 2)
        k = pl.ds(pl.multiple_of(th * 64 + tx * 16, 16), 16)
        send(xp_b.at[k], xp_in.at[j], xc_s.at[j], xc_r.at[j], (l, r, tx * 2 + th))
    own_k = pl.ds(pl.multiple_of(h * 64 + x * 16, 16), 16)
    total = xp_f[own_k, :]
    for j in range(7):
        arrive(xp_in.at[j], xc_s.at[j], xc_r.at[j])
        total = total + xp_in[j].astype(F32)
    rb_all[r] = total.astype(BF)

    for j, d in enumerate(Y_ORDER):
        send(rb_all.at[r], rb_all.at[r], rb_s.at[j], rb_r.at[j], (l, yat(d), q))
    xr_all[own_k, :] = total
    for j, (dx, dh) in enumerate(COL):
        send(xr_all.at[own_k], xr_all.at[own_k], xo_s.at[j], xo_r.at[j], (l, r, xat(dx) * 2 + lax.rem(h + dh, 2)))
    for j, d in enumerate(Y_ORDER):
        arrive(rb_all.at[yat(4 - d)], rb_s.at[j], rb_r.at[j])
    root_rows = jnp.concatenate([rb_all[t] for t in range(4)], axis=1)

    for d in Z_ORDER + (0,):
        child = zat(d)
        chosen = dot(root_rows, pick[child]).astype(BF)
        if d:
            j = Z_ORDER.index(d)
            sel_out[child] = chosen
            send(sel_out.at[child], sel_in.at[l], se_s.at[j], se_r.at[j], (child, r, q))
        else:
            sel_in[l] = chosen
    for j, (dx, dh) in enumerate(COL):
        k = pl.ds(pl.multiple_of(lax.rem(h + dh, 2) * 64 + xat(4 - dx) * 16, 16), 16)
        arrive(xr_all.at[k], xo_s.at[j], xo_r.at[j])
    flip[...] = xr_all[...].T
    xroot_ref[...] = flip[pl.ds(pl.multiple_of(q * 48, 16), 48), :]
    for d in Z_ARRIVAL:
        j = Z_ORDER.index((8 - d) % 8)
        arrive(sel_in.at[zat(d)], se_s.at[j], se_r.at[j])

    for j, (dy, dx) in enumerate(PLANE):
        send(sel_in, sel_all.at[r, x], pl_s.at[j], pl_r.at[j], (l, yat(dy), xat(dx) * 2 + h))
    sel_all[r, x] = sel_in[...]
    arrive(back_v.at[1 - h], w_s.at[0], w_r.at[0])
    arrive(bwd_v.at[1 - h], w_s.at[1], w_r.at[1])
    corr = jnp.zeros((64, 384), F32)
    for dy in (0, 1, 3, 2):
        sr = yat(dy)
        for dx in (0, 1, 3, 2):
            if dy or dx:
                j = PLANE.index(((4 - dy) % 4, (4 - dx) % 4))
                arrive(sel_all.at[sr, xat(dx)], pl_s.at[j], pl_r.at[j])
        left = jnp.concatenate([sel_all[sr, :, b].reshape(64, 128) for b in range(8)], axis=1)
        right = jnp.concatenate(
            [
                back_v[:, :, pl.ds(pl.multiple_of(b * 512 + sr * 128, 128), 128)].reshape(384, 128)
                for b in range(8)
            ],
            axis=1,
        )
        corr = corr + dot_last(left, right)
    reduced = (y_keep[...] - corr).astype(BF)

    for j, (dy, dx) in enumerate(PLANE + [(0, 0)]):
        cols = pl.ds(pl.multiple_of((yat(dy) * 4 + xat(dx)) * 384, 128), 384)
        value = dot(reduced, bwd_v[:, :, cols].reshape(384, 384))
        if dy or dx:
            z_out[j] = value.astype(BF)
            send(z_out.at[j], z_in.at[j], fin_s.at[j], fin_r.at[j], (l, yat(dy), xat(dx) * 2 + h))
    total = value
    flush()
    for j in range(14, -1, -1):
        arrive(z_in.at[j], fin_s.at[j], fin_r.at[j])
        total = total + z_in[j].astype(F32)

    zsum[mine, :] = total
    send(zsum.at[mine], zsum.at[mine], end_s.at[0], end_r.at[0], sib)
    arrive(zsum.at[other], end_s.at[0], end_r.at[0])
    flip[...] = zsum[...].T
    xchild_ref[...] = flip[pl.ds(pl.multiple_of(h * 192, 64), 192), :]
    flush()


def local(
    rhs_child, rhs_root, fwd_child, coupling, root_inverse, back_child, bwd_child, parent_rows
):
    vm = pltpu.VMEM
    dma = pltpu.SemaphoreType.DMA
    scratch = [
        vm((128, 768), BF), vm((4, 768, 384), BF), vm((1536, 512), BF), vm((1536, 384), BF),
        vm((2, 192, 4096), BF), vm((2, 192, 6144), BF), vm((32, 1536), F32), vm((8, 1, 4096), jnp.int32),
        vm((4, 128, 384), F32), vm((4, 128, 384), BF), vm((4, 64, 384), BF), vm((3, 64, 384), BF),
        vm((3, 64, 384), BF), vm((64, 384), F32), vm((4, 128, 384), BF),
        vm((128, 512), F32), vm((128, 512), BF), vm((3, 32, 512), BF), vm((8, 32, 512), BF),
        vm((8, 1536, 512), BF), vm((8, 1536, 128), BF), vm((128, 1536), BF),
        vm((128, 384), F32), vm((128, 384), BF), vm((7, 16, 384), BF), vm((128, 384), F32),
        vm((4, 16, 384), BF), vm((8, 16, 128), BF), vm((8, 16, 128), BF), vm((4, 4, 8, 16, 128), BF),
        vm((15, 64, 384), BF), vm((15, 64, 384), BF), vm((128, 384), F32), vm((384, 128), F32),
        dma((11,)),
    ]
    for n in (4, 3, 3, 4, 3, 7, 7, 3, 7, 7, 3, 7, 15, 15, 1, 2):
        scratch += [dma((n,)), dma((n,))]
    any_spec = pl.BlockSpec(memory_space=pl.ANY)
    vm_spec = pl.BlockSpec(memory_space=pltpu.VMEM)
    x_root, x_child = pl.pallas_call(
        kernel,
        out_shape=(jax.ShapeDtypeStruct((48, 128), F32), jax.ShapeDtypeStruct((192, 128), F32)),
        in_specs=[any_spec] * 8,
        out_specs=(vm_spec, vm_spec),
        scratch_shapes=scratch,
        compiler_params=pltpu.CompilerParams(
            collective_id=0, has_side_effects=True, vmem_limit_bytes=56 * 2**20
        ),
    )(
        rhs_child[0], rhs_root, fwd_child[0], coupling[0], root_inverse, back_child[0].T, bwd_child[0], parent_rows
    )
    return (x_root.T, x_child.T[None])


def solution(mesh):
    placed = (
        P("leaf", None, "col"),
        P(None, "col"),
        P("leaf", "col", "row"),
        P("leaf", "row", "col"),
        P("col", ("leaf", "row")),
        P("leaf", None, ("row", "col")),
        P("leaf", ("row", "col"), None),
        P("leaf", None),
    )
    return jax.shard_map(
        local,
        mesh=mesh,
        in_specs=placed,
        out_specs=(P(None, ("leaf", "row", "col")), P("leaf", None, ("row", "col"))),
        check_vma=False,
    )
```

time: 485 us -> 84.1 us (0.17)
  waiting for transfers between devices: 443 us -> 0 us
  Pallas kernels: 0 us -> 80.4 us
  matrix products: 21.9 us -> 0 us
  between operations: 13.9 us -> 0.64 us
    psum x3 -> x0, waiting for transfers between devices: 278 us -> none  [the longest x1 145 us: local(): lax.psum(jnp.dot(partial_u, placing, precision=lax.Precision.HIGHEST, pre...]
    reduce_scatter x1 -> x0, waiting for transfers between devices: 87.7 us -> none  [local(): lax.psum_scatter(partial_child, ('row', 'col'), scatter_dimension=1, tile...]
    pallas_call x0 -> x1, Pallas kernels: none -> 80.4 us  [local(): pl.pallas_call(kernel, out_shape=(jax.ShapeDtypeStruct((48, 128), F32), j...]
    all_gather x1 -> x0, waiting for transfers between devices: 77.3 us -> none  [local(): lax.all_gather(root_block.astype(jnp.bfloat16), ('leaf', 'row'), axis=1,...]
    dot_general x7 -> x0, matrix products: 21.9 us -> none  [the longest x5 13.6 us: product(): jnp.dot(left.astype(jnp.float32), right.astype(jnp.float32), precision=la...]
  transfers between devices with their start and end apart: 5 -> 0, of which waited for: 5 -> 0; matrix products, arithmetic and copies ran while one was open for 1% -> 0% of each run, Pallas kernels for 0% -> 0%
where the time goes in v1:
time: 84.1 us; the launch traced here: 84 us
  Pallas kernels  80.4 us (96%)
  local copies, waits for them, and re-layouts  2.89 us (3%)
    pallas_call x1, Pallas kernels, local(): pl.pallas_call(kernel, out_shape=(jax.ShapeDtypeStruct((48, 128), F32), j...  80.4 us
    unnamed x2, local copies, waits for them, and re-layouts  2.89 us

profile of v1, /device:TPU:1, one launch (start us, length us, event | category | flops | bytes accessed | tf_op | source)
XLA Modules:
  0.0 84.0 jit_solution(6454422981083092734)
XLA Ops:
  0.6 80.4 %shard_map.95 = (f32[48,128]{1,0:T(8,128)}, f32[192,128]{1,0:T(8,128)}) custom-call(bf16[128,768]{1,0:T(8,128)(2,1)} %bitcast.15, f32[128,1536]{1,0:T(8,128)} %root_ref.1, bf16[768,1536]{1,0:T(8,128)(2,1)} %bitcast.11, bf16[1536,512]{1,0:T(8,128)(2,1)} %bitcast.13, bf16[1536,384]{1,0:T(8,128)(2,1)} %rinv_ref.1, bf16[192,4096]{1,0:T(8,128)(2,1)} %bitcast.14, ...), custom_call_target="tpu_custom_call" | custom-call | tf_op jit(solution)/shard_map/pallas_call | solution.py:320
  81.1 1.3 %copy.12 = f32[128,48]{0,1:T(8,128)} copy(f32[128,48]{0,1:T(8,128)} %bitcast.17) | data formatting | bytes 49152
  82.4 1.5 %copy.13 = f32[1,128,192]{1,2,0:T(8,128)} copy(f32[1,128,192]{1,2,0:T(8,128)} %bitcast.16) | data formatting | bytes 196608

commit v2 on v1

--- a/solution.py
+++ b/solution.py
@@ -13,7 +13,7 @@
 X_ORDER = (2, 1, 3)
 Y_ORDER = (2, 1, 3)
 Z_ORDER = (4, 3, 5, 2, 6, 1, 7)
-Z_ARRIVAL = (1, 7, 2, 6, 3, 5, 4)
+Z_ARRIVAL = (4, 3, 5, 2, 6, 1, 7)
 PLANE = sorted(
     ((dy, dx) for dy in range(4) for dx in range(4) if (dy, dx) != (0, 0)),
     key=lambda p: -(min(p[0], 4 - p[0]) + min(p[1], 4 - p[1])),
@@ -31,13 +31,13 @@
 
 def kernel(
     rhs_ref, root_ref, fwd_ref, coup_ref, rinv_ref, back_ref, bwd_ref, rows_ref,
-    xroot_ref, xchild_ref,
+    both_ref,
     rhs_v, fwd_v, coup_v, rinv_v, back_v, bwd_v, root_v, rows_v,
-    part_f, part_b, core_in, x_out, x_in, y_keep, y_all,
+    part_f, part_b, core_in, x_f, x_out, x_in, y_keep,
     u_f, u_b, u_in, u_all, place, pick, p_rhs,
     xp_f, xp_b, xp_in, xr_all, rb_all, sel_out, sel_in, sel_all,
     z_out, z_in, zsum, flip,
-    load_sem, core_s, core_r, xs_s, xs_r, ag_s, ag_r, fw_s, fw_r,
+    load_sem, core_s, core_r, xs_s, xs_r,
     us_s, us_r, za_s, za_r, pr_s, pr_r, ya_s, ya_r, xc_s, xc_r, xo_s, xo_r,
     rb_s, rb_r, se_s, se_r, pl_s, pl_r, fin_s, fin_r, end_s, end_r, w_s, w_r,
 ):
@@ -79,19 +79,20 @@
 
     partners = [(l, r, xat(dx) * 2 + lax.rem(h + dh, 2)) for dx, dh in COL]
     partners += [(l, yat(dy), xat(dx) * 2 + h) for dy, dx in PLANE if dy]
+    partners += [(l, yat(d), x * 2 + 1 - h) for d in Y_ORDER]
     partners += [(zat(d), r, q) for d in Z_ORDER]
     bar = pltpu.get_barrier_semaphore()
     for p in partners:
         pl.semaphore_signal(bar, inc=1, device_id=p, device_id_type=MESH)
 
     l_rhs = load(rhs_ref, rhs_v, 0)
-    l_fwd = []
-    for j, d in enumerate(X_ORDER + (0,)):
-        cols = pl.ds(pl.multiple_of(xat(d) * 384, 128), 384)
-        l_fwd.append(load(fwd_ref.at[:, cols], fwd_v.at[j], 1 + j))
+    l_fwd = [load(fwd_ref.at[:, pl.ds(j * 384, 384)], fwd_v.at[j], 1 + j) for j in range(4)]
+    l_coup = load(coup_ref, coup_v.at[h], 6)
     l_rows = load(rows_ref, rows_v.at[l], 5)
-    l_coup = load(coup_ref, coup_v, 6)
-    l_root = load(root_ref.at[pl.ds(pl.multiple_of(r * 32, 32), 32)], root_v, 7)
+    l_root = [
+        load(root_ref.at[pl.ds(pl.multiple_of(g * 64 + r * 16, 16), 16)], root_v.at[pl.ds(g * 16, 16)], 11 + g)
+        for g in range(2)
+    ]
     l_rinv = load(rinv_ref, rinv_v, 8)
     l_back = load(back_ref, back_v.at[h], 9)
     l_bwd = load(bwd_ref, bwd_v.at[h], 10)
@@ -107,14 +108,15 @@
         if j == 0:
             pl.semaphore_wait(bar, len(partners))
         send(part_b.at[j, other], core_in.at[j], core_s.at[j], core_r.at[j], sib)
-    for j, d in enumerate(X_ORDER + (0,)):
+    l_coup.wait()
+    send(coup_v.at[h], coup_v.at[h], w_s.at[2], w_r.at[2], sib)
+    for j in range(4):
         arrive(core_in.at[j], core_s.at[j], core_r.at[j])
         both = part_f[j, mine, :] + core_in[j].astype(F32)
-        if d:
-            x_out[j] = both.astype(BF)
-            send(x_out.at[j], x_in.at[j], xs_s.at[j], xs_r.at[j], (l, r, xat(d) * 2 + h))
-        else:
-            y_keep[...] = both
+        x_f[j] = both
+        x_out[j] = both.astype(BF)
+        for i, d in enumerate(X_ORDER):
+            send(x_out.at[j], x_in.at[i, j], xs_s.at[i, j], xs_r.at[i, j], (l, r, xat(d) * 2 + h))
 
     l_rows.wait()
     for j, d in enumerate(Z_ORDER):
@@ -142,85 +144,83 @@
 
     build_place(l)
     build_pick(l)
-    for d in Z_ARRIVAL[:3]:
+    for d in Z_ARRIVAL:
         rows_arrive(d)
         build_place(zat(d))
         build_pick(zat(d))
 
-    total = y_keep[...]
-    for j in range(3):
-        arrive(x_in.at[j], xs_s.at[j], xs_r.at[j])
-        total = total + x_in[j].astype(F32)
-    y_keep[...] = total
-    y_all[x, mine, :] = total.astype(BF)
-    for j, d in enumerate(X_ORDER):
-        send(y_all.at[x, mine], y_all.at[x, mine], ag_s.at[j], ag_r.at[j], (l, r, xat(d) * 2 + h))
-    send(y_all.at[x, mine], y_all.at[x, mine], fw_s.at[3], fw_r.at[3], sib)
-    for d in Z_ARRIVAL[3:]:
-        rows_arrive(d)
-        build_place(zat(d))
-        build_pick(zat(d))
-    l_coup.wait()
-    for d in (1, 3, 2):
-        j = X_ORDER.index((4 - d) % 4)
-        src = xat(d)
-        arrive(y_all.at[src, mine], ag_s.at[j], ag_r.at[j])
-        send(y_all.at[src, mine], y_all.at[src, mine], fw_s.at[j], fw_r.at[j], sib)
-    update = jnp.zeros((128, 512), F32)
-    for d in (0, 1, 3, 2):
-        j = X_ORDER.index((4 - d) % 4) if d else 3
-        src = xat(d)
-        arrive(y_all.at[src, other], fw_s.at[j], fw_r.at[j])
-        update = update + dot(y_all[src], coup_v[pl.ds(pl.multiple_of(src * 384, 128), 384), :])
-
-    u_f[...] = update
-    u_b[...] = update.astype(BF)
-    for j, d in enumerate(Y_ORDER):
-        k = pl.ds(pl.multiple_of(yat(d) * 32, 32), 32)
-        send(u_b.at[k], u_in.at[j], us_s.at[j], us_r.at[j], (l, yat(d), q))
-    flush_before = list(pending)
-    pending.clear()
-    for c in flush_before[:-3]:
-        c.wait_send()
-    pending.extend(flush_before[-3:])
+    arrive(coup_v.at[1 - h], w_s.at[2], w_r.at[2])
+    update = [jnp.zeros((64, 512), F32) for _ in range(2)]
+    for j in range(4):
+        total = x_f[j]
+        for i in range(3):
+            arrive(x_in.at[i, j], xs_s.at[i, j], xs_r.at[i, j])
+            total = total + x_in[i, j].astype(F32)
+        x_f[j] = total
+        left = total.astype(BF)
+        for g in range(2):
+            update[g] = update[g] + dot(left, coup_v[g, pl.ds(j * 384, 384), :])
+    y_keep[...] = x_f[x]
+
+    for g in range(2):
+        u_f[g] = update[g]
+        u_b[g] = update[g].astype(BF)
+    for g in (0, 1):
+        core = lax.rem(h + g, 2)
+        for i, d in enumerate(Y_ORDER + ((0,) if g else ())):
+            k = pl.ds(pl.multiple_of(yat(d) * 16, 16), 16)
+            send(
+                u_b.at[core, k], u_in.at[g, i], us_s.at[g, i], us_r.at[g, i], (l, yat(d), x * 2 + core)
+            )
     l_back.wait()
     l_bwd.wait()
     send(back_v.at[h], back_v.at[h], w_s.at[0], w_r.at[0], sib)
     send(bwd_v.at[h], bwd_v.at[h], w_s.at[1], w_r.at[1], sib)
-    my_k = pl.ds(pl.multiple_of(r * 32, 32), 32)
-    total = u_f[my_k, :]
-    for j in range(3):
-        arrive(u_in.at[j], us_s.at[j], us_r.at[j])
-        total = total + u_in[j].astype(F32)
-    u_all[l] = total.astype(BF)
+    total = u_f[h, pl.ds(pl.multiple_of(r * 16, 16), 16), :]
+    for i in range(3):
+        arrive(u_in.at[0, i], us_s.at[0, i], us_r.at[0, i])
+        total = total + u_in[0, i].astype(F32)
+    u_all[l, pl.ds(pl.multiple_of(h * 16, 16), 16), :] = total.astype(BF)
+    total = jnp.zeros((16, 512), F32)
+    for i in range(4):
+        arrive(u_in.at[1, i], us_s.at[1, i], us_r.at[1, i])
+        total = total + u_in[1, i].astype(F32)
+    u_all[l, pl.ds(pl.multiple_of((1 - h) * 16, 16), 16), :] = total.astype(BF)
 
     for j, d in enumerate(Z_ORDER):
         send(u_all.at[l], u_all.at[l], za_s.at[j], za_r.at[j], (zat(d), r, q))
-    l_root.wait()
-    placed = dot_last(u_all[l], place[l])
-    for d in Z_ARRIVAL:
+    for c in l_root:
+        c.wait()
+    placed = root_v[...] - dot_last(u_all[l], place[l])
+    for d in Z_ARRIVAL[:6]:
         j = Z_ORDER.index((8 - d) % 8)
         leaf = zat(d)
         arrive(u_all.at[leaf], za_s.at[j], za_r.at[j])
-        placed = placed + dot_last(u_all[leaf], place[leaf])
-    p_rhs[my_k, :] = (root_v[...] - placed).astype(BF)
-
-    for j, d in enumerate(Y_ORDER):
-        send(p_rhs.at[my_k], p_rhs.at[my_k], ya_s.at[j], ya_r.at[j], (l, yat(d), q))
+        placed = placed - dot_last(u_all[leaf], place[leaf])
+    d = Z_ARRIVAL[6]
+    leaf = zat(d)
+    arrive(u_all.at[leaf], za_s.at[Z_ORDER.index((8 - d) % 8)], za_r.at[Z_ORDER.index((8 - d) % 8)])
+
+    for t in range(2):
+        cols = slice(t * 768, t * 768 + 768)
+        p_rhs[t, r] = (placed[:, cols] - dot_last(u_all[leaf], place[leaf, cols, :])).astype(BF)
+        for i, d in enumerate(Y_ORDER):
+            send(p_rhs.at[t, r], p_rhs.at[t, r], ya_s.at[t, i], ya_r.at[t, i], (l, yat(d), q))
     l_rinv.wait()
-    for j, d in enumerate(Y_ORDER):
-        k = pl.ds(pl.multiple_of(yat(4 - d) * 32, 32), 32)
-        arrive(p_rhs.at[k], ya_s.at[j], ya_r.at[j])
-    value = dot(p_rhs[...], rinv_v[...])
+    value = jnp.zeros((128, 384), F32)
+    for t in range(2):
+        for i, d in enumerate(Y_ORDER):
+            arrive(p_rhs.at[t, yat(4 - d)], ya_s.at[t, i], ya_r.at[t, i])
+        value = value + dot(p_rhs[t].reshape(128, 768), rinv_v[pl.ds(t * 768, 768), :])
 
     xp_f[...] = value
     xp_b[...] = value.astype(BF)
     for j, (dx, dh) in enumerate(COL):
         tx, th = xat(dx), lax.rem(h + dh, 2)
-        k = pl.ds(pl.multiple_of(th * 64 + tx * 16, 16), 16)
+        k = pl.ds(pl.multiple_of(tx * 32 + th * 16, 16), 16)
         send(xp_b.at[k], xp_in.at[j], xc_s.at[j], xc_r.at[j], (l, r, tx * 2 + th))
     own_k = pl.ds(pl.multiple_of(h * 64 + x * 16, 16), 16)
-    total = xp_f[own_k, :]
+    total = xp_f[pl.ds(pl.multiple_of(x * 32 + h * 16, 16), 16), :]
     for j in range(7):
         arrive(xp_in.at[j], xc_s.at[j], xc_r.at[j])
         total = total + xp_in[j].astype(F32)
@@ -248,7 +248,7 @@
         k = pl.ds(pl.multiple_of(lax.rem(h + dh, 2) * 64 + xat(4 - dx) * 16, 16), 16)
         arrive(xr_all.at[k], xo_s.at[j], xo_r.at[j])
     flip[...] = xr_all[...].T
-    xroot_ref[...] = flip[pl.ds(pl.multiple_of(q * 48, 16), 48), :]
+    both_ref[0:48, :] = flip[pl.ds(pl.multiple_of(q * 48, 16), 48), :]
     for d in Z_ARRIVAL:
         j = Z_ORDER.index((8 - d) % 8)
         arrive(sel_in.at[zat(d)], se_s.at[j], se_r.at[j])
@@ -292,8 +292,13 @@
     send(zsum.at[mine], zsum.at[mine], end_s.at[0], end_r.at[0], sib)
     arrive(zsum.at[other], end_s.at[0], end_r.at[0])
     flip[...] = zsum[...].T
-    xchild_ref[...] = flip[pl.ds(pl.multiple_of(h * 192, 64), 192), :]
+    both_ref[48:240, :] = flip[pl.ds(pl.multiple_of(h * 192, 64), 192), :]
     flush()
+
+
+def split(both_ref, xroot_ref, xchild_ref):
+    xroot_ref[...] = both_ref[0:48, :]
+    xchild_ref[...] = both_ref[48:240, :]
 
 
 def local(
@@ -302,26 +307,27 @@
     vm = pltpu.VMEM
     dma = pltpu.SemaphoreType.DMA
     scratch = [
-        vm((128, 768), BF), vm((4, 768, 384), BF), vm((1536, 512), BF), vm((1536, 384), BF),
+        vm((128, 768), BF), vm((4, 768, 384), BF), vm((2, 1536, 512), BF), vm((1536, 384), BF),
         vm((2, 192, 4096), BF), vm((2, 192, 6144), BF), vm((32, 1536), F32), vm((8, 1, 4096), jnp.int32),
-        vm((4, 128, 384), F32), vm((4, 128, 384), BF), vm((4, 64, 384), BF), vm((3, 64, 384), BF),
-        vm((3, 64, 384), BF), vm((64, 384), F32), vm((4, 128, 384), BF),
-        vm((128, 512), F32), vm((128, 512), BF), vm((3, 32, 512), BF), vm((8, 32, 512), BF),
-        vm((8, 1536, 512), BF), vm((8, 1536, 128), BF), vm((128, 1536), BF),
+        vm((4, 128, 384), F32), vm((4, 128, 384), BF), vm((4, 64, 384), BF), vm((4, 64, 384), F32),
+        vm((4, 64, 384), BF), vm((3, 4, 64, 384), BF), vm((64, 384), F32),
+        vm((2, 64, 512), F32), vm((2, 64, 512), BF), vm((2, 4, 16, 512), BF), vm((8, 32, 512), BF),
+        vm((8, 1536, 512), BF), vm((8, 1536, 128), BF), vm((2, 4, 32, 768), BF),
         vm((128, 384), F32), vm((128, 384), BF), vm((7, 16, 384), BF), vm((128, 384), F32),
         vm((4, 16, 384), BF), vm((8, 16, 128), BF), vm((8, 16, 128), BF), vm((4, 4, 8, 16, 128), BF),
         vm((15, 64, 384), BF), vm((15, 64, 384), BF), vm((128, 384), F32), vm((384, 128), F32),
-        dma((11,)),
+        dma((13,)),
     ]
-    for n in (4, 3, 3, 4, 3, 7, 7, 3, 7, 7, 3, 7, 15, 15, 1, 2):
-        scratch += [dma((n,)), dma((n,))]
+    for n in (4, (3, 4), (2, 4), 7, 7, (2, 3), 7, 7, 3, 7, 15, 15, 1, 3):
+        n = n if isinstance(n, tuple) else (n,)
+        scratch += [dma(n), dma(n)]
     any_spec = pl.BlockSpec(memory_space=pl.ANY)
     vm_spec = pl.BlockSpec(memory_space=pltpu.VMEM)
-    x_root, x_child = pl.pallas_call(
+    both = pl.pallas_call(
         kernel,
-        out_shape=(jax.ShapeDtypeStruct((48, 128), F32), jax.ShapeDtypeStruct((192, 128), F32)),
+        out_shape=jax.ShapeDtypeStruct((240, 128), F32),
         in_specs=[any_spec] * 8,
-        out_specs=(vm_spec, vm_spec),
+        out_specs=vm_spec,
         scratch_shapes=scratch,
         compiler_params=pltpu.CompilerParams(
             collective_id=0, has_side_effects=True, vmem_limit_bytes=56 * 2**20
@@ -329,6 +335,12 @@
     )(
         rhs_child[0], rhs_root, fwd_child[0], coupling[0], root_inverse, back_child[0].T, bwd_child[0], parent_rows
     )
+    x_root, x_child = pl.pallas_call(
+        split,
+        out_shape=(jax.ShapeDtypeStruct((48, 128), F32), jax.ShapeDtypeStruct((192, 128), F32)),
+        in_specs=[vm_spec],
+        out_specs=(vm_spec, vm_spec),
+    )(both)
     return (x_root.T, x_child.T[None])
 
 

time: 84.1 us -> 78.6 us (0.935)
  local copies, waits for them, and re-layouts: 2.89 us -> 0 us
  Pallas kernels: 80.4 us -> 77.8 us
    unnamed x2 -> x0, local copies, waits for them, and re-layouts: 2.89 us -> none
    pallas_call x1 -> x2, Pallas kernels: 80.4 us -> 77.8 us  [the longest x1 76.3 us: local(): pl.pallas_call(kernel, out_shape=jax.ShapeDtypeStruct((240, 128), F32), i...]
where the time goes in v2:
time: 78.6 us; the launch traced here: 78.5 us
  Pallas kernels  77.8 us (99%)
    pallas_call x1, Pallas kernels, local(): pl.pallas_call(kernel, out_shape=jax.ShapeDtypeStruct((240, 128), F32), i...  76.3 us

profile of v2, /device:TPU:1, one launch (start us, length us, event | category | flops | bytes accessed | tf_op | source)
XLA Modules:
  0.0 78.5 jit_solution(13642984979324812015)
XLA Ops:
  0.6 76.3 %shard_map.95.both_ref = f32[240,128]{1,0:T(8,128)} custom-call(bf16[128,768]{1,0:T(8,128)(2,1)} %bitcast.15, f32[128,1536]{1,0:T(8,128)} %root_ref.1, bf16[768,1536]{1,0:T(8,128)(2,1)} %bitcast.11, bf16[1536,512]{1,0:T(8,128)(2,1)} %bitcast.13, bf16[1536,384]{1,0:T(8,128)(2,1)} %rinv_ref.1, bf16[192,4096]{1,0:T(8,128)(2,1)} %bitcast.14, ...), custom_call_target="tpu_custom_call" | custom-call | tf_op jit(solution)/shard_map/pallas_call | solution.py:326
  76.9 1.6 %shard_map.96 = (f32[48,128]{1,0:T(8,128)}, f32[192,128]{1,0:T(8,128)}) custom-call(f32[240,128]{1,0:T(8,128)} %shard_map.95.both_ref), custom_call_target="tpu_custom_call" | custom-call | tf_op jit(solution)/shard_map/pallas_call | solution.py:338

commit v3 on v2

--- a/solution.py
+++ b/solution.py
@@ -18,6 +18,10 @@
     ((dy, dx) for dy in range(4) for dx in range(4) if (dy, dx) != (0, 0)),
     key=lambda p: -(min(p[0], 4 - p[0]) + min(p[1], 4 - p[1])),
 )
+OWNERS = (
+    (2, 2), (2, 1), (1, 2), (2, 3), (3, 2), (2, 0), (0, 2),
+    (1, 1), (1, 3), (3, 1), (1, 0), (0, 1), (3, 3), (3, 0), (0, 3), (0, 0),
+)
 COL = [(dx, dh) for dx in (2, 1, 3) for dh in (1, 0)] + [(0, 1)]
 
 
@@ -36,10 +40,10 @@
     part_f, part_b, core_in, x_f, x_out, x_in, y_keep,
     u_f, u_b, u_in, u_all, place, pick, p_rhs,
     xp_f, xp_b, xp_in, xr_all, rb_all, sel_out, sel_in, sel_all,
-    z_out, z_in, zsum, flip,
+    z_out, a_f, b_f, a_in, b_in, a_out, b_out, fa_in, fb_in, own_f, own_in, flip, flip2,
     load_sem, core_s, core_r, xs_s, xs_r,
     us_s, us_r, za_s, za_r, pr_s, pr_r, ya_s, ya_r, xc_s, xc_r, xo_s, xo_r,
-    rb_s, rb_r, se_s, se_r, pl_s, pl_r, fin_s, fin_r, end_s, end_r, w_s, w_r,
+    rb_s, rb_r, se_s, se_r, pl_s, pl_r, a_s, a_r, b_s, b_r, fa_s, fa_r, fb_s, fb_r, end_s, end_r, w_s, w_r,
 ):
     l, r, q = lax.axis_index("leaf"), lax.axis_index("row"), lax.axis_index("col")
     x, h = q // 2, q % 2
@@ -77,6 +81,8 @@
         while pending:
             pending.pop(0).wait_send()
 
+    l_rhs = load(rhs_ref, rhs_v, 0)
+    l_fwd = [load(fwd_ref.at[:, pl.ds(j * 384, 384)], fwd_v.at[j], 1 + j) for j in range(4)]
     partners = [(l, r, xat(dx) * 2 + lax.rem(h + dh, 2)) for dx, dh in COL]
     partners += [(l, yat(dy), xat(dx) * 2 + h) for dy, dx in PLANE if dy]
     partners += [(l, yat(d), x * 2 + 1 - h) for d in Y_ORDER]
@@ -85,17 +91,8 @@
     for p in partners:
         pl.semaphore_signal(bar, inc=1, device_id=p, device_id_type=MESH)
 
-    l_rhs = load(rhs_ref, rhs_v, 0)
-    l_fwd = [load(fwd_ref.at[:, pl.ds(j * 384, 384)], fwd_v.at[j], 1 + j) for j in range(4)]
     l_coup = load(coup_ref, coup_v.at[h], 6)
     l_rows = load(rows_ref, rows_v.at[l], 5)
-    l_root = [
-        load(root_ref.at[pl.ds(pl.multiple_of(g * 64 + r * 16, 16), 16)], root_v.at[pl.ds(g * 16, 16)], 11 + g)
-        for g in range(2)
-    ]
-    l_rinv = load(rinv_ref, rinv_v, 8)
-    l_back = load(back_ref, back_v.at[h], 9)
-    l_bwd = load(bwd_ref, bwd_v.at[h], 10)
 
     mine = pl.ds(pl.multiple_of(h * 64, 64), 64)
     other = pl.ds(pl.multiple_of((1 - h) * 64, 64), 64)
@@ -108,6 +105,13 @@
         if j == 0:
             pl.semaphore_wait(bar, len(partners))
         send(part_b.at[j, other], core_in.at[j], core_s.at[j], core_r.at[j], sib)
+    l_root = [
+        load(root_ref.at[pl.ds(pl.multiple_of(g * 64 + r * 16, 16), 16)], root_v.at[pl.ds(g * 16, 16)], 11 + g)
+        for g in range(2)
+    ]
+    l_rinv = load(rinv_ref, rinv_v, 8)
+    l_back = load(back_ref, back_v.at[h], 9)
+    l_bwd = load(bwd_ref, bwd_v.at[h], 10)
     l_coup.wait()
     send(coup_v.at[h], coup_v.at[h], w_s.at[2], w_r.at[2], sib)
     for j in range(4):
@@ -143,11 +147,9 @@
         arrive(rows_v.at[zat(d)], pr_s.at[j], pr_r.at[j])
 
     build_place(l)
-    build_pick(l)
-    for d in Z_ARRIVAL:
+    for d in (1, 7, 2, 6):
         rows_arrive(d)
         build_place(zat(d))
-        build_pick(zat(d))
 
     arrive(coup_v.at[1 - h], w_s.at[2], w_r.at[2])
     update = [jnp.zeros((64, 512), F32) for _ in range(2)]
@@ -176,6 +178,9 @@
     l_bwd.wait()
     send(back_v.at[h], back_v.at[h], w_s.at[0], w_r.at[0], sib)
     send(bwd_v.at[h], bwd_v.at[h], w_s.at[1], w_r.at[1], sib)
+    for d in (3, 5, 4):
+        rows_arrive(d)
+        build_place(zat(d))
     total = u_f[h, pl.ds(pl.multiple_of(r * 16, 16), 16), :]
     for i in range(3):
         arrive(u_in.at[0, i], us_s.at[0, i], us_r.at[0, i])
@@ -206,6 +211,8 @@
         p_rhs[t, r] = (placed[:, cols] - dot_last(u_all[leaf], place[leaf, cols, :])).astype(BF)
         for i, d in enumerate(Y_ORDER):
             send(p_rhs.at[t, r], p_rhs.at[t, r], ya_s.at[t, i], ya_r.at[t, i], (l, yat(d), q))
+    for d in range(8):
+        build_pick(zat(d))
     l_rinv.wait()
     value = jnp.zeros((128, 384), F32)
     for t in range(2):
@@ -276,24 +283,50 @@
         corr = corr + dot_last(left, right)
     reduced = (y_keep[...] - corr).astype(BF)
 
-    for j, (dy, dx) in enumerate(PLANE + [(0, 0)]):
+    for j, (dy, dx) in enumerate(OWNERS):
         cols = pl.ds(pl.multiple_of((yat(dy) * 4 + xat(dx)) * 384, 128), 384)
         value = dot(reduced, bwd_v[:, :, cols].reshape(384, 384))
-        if dy or dx:
-            z_out[j] = value.astype(BF)
-            send(z_out.at[j], z_in.at[j], fin_s.at[j], fin_r.at[j], (l, yat(dy), xat(dx) * 2 + h))
-    total = value
+        z_out[j] = value.astype(BF)
+        if dx:
+            send(z_out.at[j, 0:32], a_in.at[dy, dx - 1], a_s.at[dy, dx - 1], a_r.at[dy, dx - 1], (l, r, xat(dx) * 2 + h))
+        else:
+            a_f[dy] = value[0:32]
+        if dy:
+            send(z_out.at[j, 32:64], b_in.at[dx, dy - 1], b_s.at[dx, dy - 1], b_r.at[dx, dy - 1], (l, yat(dy), x * 2 + h))
+        else:
+            b_f[dx] = value[32:64]
+    for c in pending[:-24]:
+        c.wait_send()
+    del pending[:-24]
+    for d in (2, 1, 3, 0):
+        for first, came, s_sem, r_sem, on, fin, fin_s, fin_r, at in (
+            (a_f, a_in, a_s, a_r, a_out, fa_in, fa_s, fa_r, 0), (b_f, b_in, b_s, b_r, b_out, fb_in, fb_s, fb_r, 32)
+        ):
+            total = first[d]
+            for i in range(3):
+                arrive(came.at[d, i], s_sem.at[d, i], r_sem.at[d, i])
+                total = total + came[d, i].astype(F32)
+            if d:
+                on[d - 1] = total.astype(BF)
+                for g in range(2):
+                    to = (l, r, xat(d) * 2 + g) if at else (l, yat(d), x * 2 + g)
+                    send(on.at[d - 1, :, g * 128 : g * 128 + 256], fin.at[h, d - 1], fin_s.at[g, d - 1], fin_r.at[h, d - 1], to)
+            else:
+                own_f[at : at + 32, :] = total
+
+    send(
+        own_f.at[:, pl.ds(pl.multiple_of((1 - h) * 128, 128), 256)], own_in.at[h], end_s.at[0], end_r.at[0], sib
+    )
+    own_in[h] = own_f[:, pl.ds(pl.multiple_of(h * 128, 128), 256)]
     flush()
-    for j in range(14, -1, -1):
-        arrive(z_in.at[j], fin_s.at[j], fin_r.at[j])
-        total = total + z_in[j].astype(F32)
-
-    zsum[mine, :] = total
-    send(zsum.at[mine], zsum.at[mine], end_s.at[0], end_r.at[0], sib)
-    arrive(zsum.at[other], end_s.at[0], end_r.at[0])
-    flip[...] = zsum[...].T
-    both_ref[48:240, :] = flip[pl.ds(pl.multiple_of(h * 192, 64), 192), :]
-    flush()
+    arrive(own_in.at[1 - h], end_s.at[0], end_r.at[0])
+    for d in (2, 1, 3):
+        for fin, fin_s, fin_r, at in ((fa_in, fa_s, fa_r, 0), (fb_in, fb_s, fb_r, 32)):
+            for c in range(2):
+                arrive(fin.at[c, d - 1], fin_s.at[c, d - 1], fin_r.at[c, d - 1])
+                own_in[c, at : at + 32] = own_in[c, at : at + 32] + fin[c, d - 1].astype(F32)
+    flip2[...] = own_in[...].reshape(128, 256).T
+    both_ref[48:240, :] = flip2[pl.ds(pl.multiple_of(h * 64, 64), 192), :]
 
 
 def split(both_ref, xroot_ref, xchild_ref):
@@ -315,10 +348,13 @@
         vm((8, 1536, 512), BF), vm((8, 1536, 128), BF), vm((2, 4, 32, 768), BF),
         vm((128, 384), F32), vm((128, 384), BF), vm((7, 16, 384), BF), vm((128, 384), F32),
         vm((4, 16, 384), BF), vm((8, 16, 128), BF), vm((8, 16, 128), BF), vm((4, 4, 8, 16, 128), BF),
-        vm((15, 64, 384), BF), vm((15, 64, 384), BF), vm((128, 384), F32), vm((384, 128), F32),
+        vm((16, 64, 384), BF), vm((4, 32, 384), F32), vm((4, 32, 384), F32),
+        vm((4, 3, 32, 384), BF), vm((4, 3, 32, 384), BF), vm((3, 32, 384), BF), vm((3, 32, 384), BF),
+        vm((2, 3, 32, 256), BF), vm((2, 3, 32, 256), BF), vm((64, 384), F32), vm((2, 64, 256), F32),
+        vm((384, 128), F32), vm((256, 128), F32),
         dma((13,)),
     ]
-    for n in (4, (3, 4), (2, 4), 7, 7, (2, 3), 7, 7, 3, 7, 15, 15, 1, 3):
+    for n in (4, (3, 4), (2, 4), 7, 7, (2, 3), 7, 7, 3, 7, 15, (4, 3), (4, 3), (2, 3), (2, 3), 1, 3):
         n = n if isinstance(n, tuple) else (n,)
         scratch += [dma(n), dma(n)]
     any_spec = pl.BlockSpec(memory_space=pl.ANY)

time: 78.6 us -> 77.4 us (0.985)
  Pallas kernels: 77.8 us -> 76.6 us
    pallas_call x1, Pallas kernels: 76.3 us -> 75.1 us  [local(): pl.pallas_call(kernel, out_shape=jax.ShapeDtypeStruct((240, 128), F32), i...]
where the time goes in v3:
time: 77.4 us; the launch traced here: 77.3 us
  Pallas kernels  76.6 us (99%)
    pallas_call x1, Pallas kernels, local(): pl.pallas_call(kernel, out_shape=jax.ShapeDtypeStruct((240, 128), F32), i...  75.1 us
    pallas_call x1, Pallas kernels, local(): pl.pallas_call(split, out_shape=(jax.ShapeDtypeStruct((48, 128), F32), ja...  1.55 us

profile of v3, /device:TPU:1, one launch (start us, length us, event | category | flops | bytes accessed | tf_op | source)
XLA Modules:
  0.0 77.3 jit_solution(1677637528092923664)
XLA Ops:
  0.6 75.1 %shard_map.95.both_ref = f32[240,128]{1,0:T(8,128)} custom-call(bf16[128,768]{1,0:T(8,128)(2,1)} %bitcast.15, f32[128,1536]{1,0:T(8,128)} %root_ref.1, bf16[768,1536]{1,0:T(8,128)(2,1)} %bitcast.11, bf16[1536,512]{1,0:T(8,128)(2,1)} %bitcast.13, bf16[1536,384]{1,0:T(8,128)(2,1)} %rinv_ref.1, bf16[192,4096]{1,0:T(8,128)(2,1)} %bitcast.14, ...), custom_call_target="tpu_custom_call" | custom-call | tf_op jit(solution)/shard_map/pallas_call | solution.py:362
  75.7 1.6 %shard_map.96 = (f32[48,128]{1,0:T(8,128)}, f32[192,128]{1,0:T(8,128)}) custom-call(f32[240,128]{1,0:T(8,128)} %shard_map.95.both_ref), custom_call_target="tpu_custom_call" | custom-call | tf_op jit(solution)/shard_map/pallas_call | solution.py:374

commit v4 on v3

--- a/solution.py
+++ b/solution.py
@@ -11,6 +11,9 @@
 CONTRACT_LAST = (((1,), (1,)), ((), ()))
 
 X_ORDER = (2, 1, 3)
+NEAR = (0, 1, 7, 2, 6, 3, 5, 4)
+GROUPS = ((0, 5), (5, 8))
+X_BLOCKS = X_ORDER + (0,)
 Y_ORDER = (2, 1, 3)
 Z_ORDER = (4, 3, 5, 2, 6, 1, 7)
 Z_ARRIVAL = (4, 3, 5, 2, 6, 1, 7)
@@ -37,11 +40,11 @@
     rhs_ref, root_ref, fwd_ref, coup_ref, rinv_ref, back_ref, bwd_ref, rows_ref,
     both_ref,
     rhs_v, fwd_v, coup_v, rinv_v, back_v, bwd_v, root_v, rows_v,
-    part_f, part_b, core_in, x_f, x_out, x_in, y_keep,
+    part_f, part_b, core_in, x_f, x_out, x_in, rs_in, ag, y_keep,
     u_f, u_b, u_in, u_all, place, pick, p_rhs,
     xp_f, xp_b, xp_in, xr_all, rb_all, sel_out, sel_in, sel_all,
     z_out, a_f, b_f, a_in, b_in, a_out, b_out, fa_in, fb_in, own_f, own_in, flip, flip2,
-    load_sem, core_s, core_r, xs_s, xs_r,
+    load_sem, core_s, core_r, xs_s, xs_r, rs_s, rs_r, ag_s, ag_r,
     us_s, us_r, za_s, za_r, pr_s, pr_r, ya_s, ya_r, xc_s, xc_r, xo_s, xo_r,
     rb_s, rb_r, se_s, se_r, pl_s, pl_r, a_s, a_r, b_s, b_r, fa_s, fa_r, fb_s, fb_r, end_s, end_r, w_s, w_r,
 ):
@@ -82,7 +85,10 @@
             pending.pop(0).wait_send()
 
     l_rhs = load(rhs_ref, rhs_v, 0)
-    l_fwd = [load(fwd_ref.at[:, pl.ds(j * 384, 384)], fwd_v.at[j], 1 + j) for j in range(4)]
+    l_fwd = []
+    for j, d in enumerate(X_BLOCKS):
+        cols = pl.ds(pl.multiple_of(xat(d) * 384, 128), 384)
+        l_fwd.append(load(fwd_ref.at[:, cols], fwd_v.at[j], 1 + j))
     partners = [(l, r, xat(dx) * 2 + lax.rem(h + dh, 2)) for dx, dh in COL]
     partners += [(l, yat(dy), xat(dx) * 2 + h) for dy, dx in PLANE if dy]
     partners += [(l, yat(d), x * 2 + 1 - h) for d in Y_ORDER]
@@ -114,13 +120,17 @@
     l_bwd = load(bwd_ref, bwd_v.at[h], 10)
     l_coup.wait()
     send(coup_v.at[h], coup_v.at[h], w_s.at[2], w_r.at[2], sib)
-    for j in range(4):
+    for j, d in enumerate(X_BLOCKS):
         arrive(core_in.at[j], core_s.at[j], core_r.at[j])
         both = part_f[j, mine, :] + core_in[j].astype(F32)
         x_f[j] = both
         x_out[j] = both.astype(BF)
-        for i, d in enumerate(X_ORDER):
-            send(x_out.at[j], x_in.at[i, j], xs_s.at[i, j], xs_r.at[i, j], (l, r, xat(d) * 2 + h))
+        if d:
+            send(x_out.at[j, 32:64], rs_in.at[j], rs_s.at[j], rs_r.at[j], (l, r, xat(d) * 2 + h))
+    for j, d in enumerate(X_BLOCKS):
+        for i, e in enumerate(X_ORDER):
+            block = xat(d)
+            send(x_out.at[j, 0:32], x_in.at[i, block], xs_s.at[i, j], xs_r.at[i, block], (l, r, xat(e) * 2 + h))
 
     l_rows.wait()
     for j, d in enumerate(Z_ORDER):
@@ -147,22 +157,35 @@
         arrive(rows_v.at[zat(d)], pr_s.at[j], pr_r.at[j])
 
     build_place(l)
+
+    total = x_f[3, 32:64, :]
+    for i in range(3):
+        arrive(rs_in.at[i], rs_s.at[i], rs_r.at[i])
+        total = total + rs_in[i].astype(F32)
+    y_keep[32:64, :] = total
+    ag[x] = total.astype(BF)
+    for i, e in enumerate(X_ORDER):
+        send(ag.at[x], ag.at[x], ag_s.at[i], ag_r.at[i], (l, r, xat(e) * 2 + h))
     for d in (1, 7, 2, 6):
         rows_arrive(d)
         build_place(zat(d))
 
     arrive(coup_v.at[1 - h], w_s.at[2], w_r.at[2])
     update = [jnp.zeros((64, 512), F32) for _ in range(2)]
-    for j in range(4):
-        total = x_f[j]
+    for d in (0, 1, 3, 2):
+        block = xat(d)
+        total = x_f[X_BLOCKS.index(d), 0:32, :]
         for i in range(3):
-            arrive(x_in.at[i, j], xs_s.at[i, j], xs_r.at[i, j])
-            total = total + x_in[i, j].astype(F32)
-        x_f[j] = total
-        left = total.astype(BF)
+            arrive(x_in.at[i, block], xs_s.at[i, 0], xs_r.at[i, block])
+            total = total + x_in[i, block].astype(F32)
+        if d:
+            i = X_ORDER.index((4 - d) % 4)
+            arrive(ag.at[block], ag_s.at[i], ag_r.at[i])
+        else:
+            y_keep[0:32, :] = total
+        left = jnp.concatenate([total.astype(BF), ag[block]], axis=0)
         for g in range(2):
-            update[g] = update[g] + dot(left, coup_v[g, pl.ds(j * 384, 384), :])
-    y_keep[...] = x_f[x]
+            update[g] = update[g] + dot(left, coup_v[g, pl.ds(pl.multiple_of(block * 384, 128), 384), :])
 
     for g in range(2):
         u_f[g] = update[g]
@@ -248,39 +271,43 @@
         if d:
             j = Z_ORDER.index(d)
             sel_out[child] = chosen
-            send(sel_out.at[child], sel_in.at[l], se_s.at[j], se_r.at[j], (child, r, q))
+            send(sel_out.at[child], sel_in.at[NEAR.index(8 - d)], se_s.at[j], se_r.at[j], (child, r, q))
         else:
-            sel_in[l] = chosen
+            sel_in[0] = chosen
     for j, (dx, dh) in enumerate(COL):
         k = pl.ds(pl.multiple_of(lax.rem(h + dh, 2) * 64 + xat(4 - dx) * 16, 16), 16)
         arrive(xr_all.at[k], xo_s.at[j], xo_r.at[j])
     flip[...] = xr_all[...].T
     both_ref[0:48, :] = flip[pl.ds(pl.multiple_of(q * 48, 16), 48), :]
-    for d in Z_ARRIVAL:
-        j = Z_ORDER.index((8 - d) % 8)
-        arrive(sel_in.at[zat(d)], se_s.at[j], se_r.at[j])
-
-    for j, (dy, dx) in enumerate(PLANE):
-        send(sel_in, sel_all.at[r, x], pl_s.at[j], pl_r.at[j], (l, yat(dy), xat(dx) * 2 + h))
-    sel_all[r, x] = sel_in[...]
+
+    for g, (low, high) in enumerate(GROUPS):
+        for n in range(max(low, 1), high):
+            j = Z_ORDER.index(8 - NEAR[n])
+            arrive(sel_in.at[n], se_s.at[j], se_r.at[j])
+        for j, (dy, dx) in enumerate(PLANE):
+            send(
+                sel_in.at[low:high], sel_all.at[r, x, low:high], pl_s.at[g, j], pl_r.at[g, j], (l, yat(dy), xat(dx) * 2 + h)
+            )
+        sel_all[r, x, low:high] = sel_in[low:high]
     arrive(back_v.at[1 - h], w_s.at[0], w_r.at[0])
     arrive(bwd_v.at[1 - h], w_s.at[1], w_r.at[1])
     corr = jnp.zeros((64, 384), F32)
-    for dy in (0, 1, 3, 2):
-        sr = yat(dy)
-        for dx in (0, 1, 3, 2):
-            if dy or dx:
-                j = PLANE.index(((4 - dy) % 4, (4 - dx) % 4))
-                arrive(sel_all.at[sr, xat(dx)], pl_s.at[j], pl_r.at[j])
-        left = jnp.concatenate([sel_all[sr, :, b].reshape(64, 128) for b in range(8)], axis=1)
-        right = jnp.concatenate(
-            [
-                back_v[:, :, pl.ds(pl.multiple_of(b * 512 + sr * 128, 128), 128)].reshape(384, 128)
-                for b in range(8)
-            ],
-            axis=1,
-        )
-        corr = corr + dot_last(left, right)
+    for g, (low, high) in enumerate(GROUPS):
+        for dy in (0, 1, 3, 2):
+            sr = yat(dy)
+            for dx in (0, 1, 3, 2):
+                if dy or dx:
+                    j = PLANE.index(((4 - dy) % 4, (4 - dx) % 4))
+                    arrive(sel_all.at[sr, xat(dx), low:high], pl_s.at[g, j], pl_r.at[g, j])
+            left = jnp.concatenate([sel_all[sr, :, n].reshape(64, 128) for n in range(low, high)], axis=1)
+            right = jnp.concatenate(
+                [
+                    back_v[:, :, pl.ds(pl.multiple_of(zat(NEAR[n]) * 512 + sr * 128, 128), 128)].reshape(384, 128)
+                    for n in range(low, high)
+                ],
+                axis=1,
+            )
+            corr = corr + dot_last(left, right)
     reduced = (y_keep[...] - corr).astype(BF)
 
     for j, (dy, dx) in enumerate(OWNERS):
@@ -343,7 +370,7 @@
         vm((128, 768), BF), vm((4, 768, 384), BF), vm((2, 1536, 512), BF), vm((1536, 384), BF),
         vm((2, 192, 4096), BF), vm((2, 192, 6144), BF), vm((32, 1536), F32), vm((8, 1, 4096), jnp.int32),
         vm((4, 128, 384), F32), vm((4, 128, 384), BF), vm((4, 64, 384), BF), vm((4, 64, 384), F32),
-        vm((4, 64, 384), BF), vm((3, 4, 64, 384), BF), vm((64, 384), F32),
+        vm((4, 64, 384), BF), vm((3, 4, 32, 384), BF), vm((3, 32, 384), BF), vm((4, 32, 384), BF), vm((64, 384), F32),
         vm((2, 64, 512), F32), vm((2, 64, 512), BF), vm((2, 4, 16, 512), BF), vm((8, 32, 512), BF),
         vm((8, 1536, 512), BF), vm((8, 1536, 128), BF), vm((2, 4, 32, 768), BF),
         vm((128, 384), F32), vm((128, 384), BF), vm((7, 16, 384), BF), vm((128, 384), F32),
@@ -354,14 +381,14 @@
         vm((384, 128), F32), vm((256, 128), F32),
         dma((13,)),
     ]
-    for n in (4, (3, 4), (2, 4), 7, 7, (2, 3), 7, 7, 3, 7, 15, (4, 3), (4, 3), (2, 3), (2, 3), 1, 3):
+    for n in (4, (3, 4), 3, 3, (2, 4), 7, 7, (2, 3), 7, 7, 3, 7, (2, 15), (4, 3), (4, 3), (2, 3), (2, 3), 1, 3):
         n = n if isinstance(n, tuple) else (n,)
         scratch += [dma(n), dma(n)]
     any_spec = pl.BlockSpec(memory_space=pl.ANY)
     vm_spec = pl.BlockSpec(memory_space=pltpu.VMEM)
     both = pl.pallas_call(
         kernel,
-        out_shape=jax.ShapeDtypeStruct((240, 128), F32),
+        out_shape=pltpu.VMEM((240, 128), F32),
         in_specs=[any_spec] * 8,
         out_specs=vm_spec,
         scratch_shapes=scratch,
@@ -376,7 +403,7 @@
         out_shape=(jax.ShapeDtypeStruct((48, 128), F32), jax.ShapeDtypeStruct((192, 128), F32)),
         in_specs=[vm_spec],
         out_specs=(vm_spec, vm_spec),
-    )(both)
+    )(pltpu.with_memory_space_constraint(both, pltpu.VMEM))
     return (x_root.T, x_child.T[None])
 
 

time: 77.4 us -> 74.2 us (0.959)
  Pallas kernels: 76.6 us -> 73.5 us
    pallas_call x1, Pallas kernels: 75.1 us -> 72.8 us  [local(): pl.pallas_call(kernel, out_shape=pltpu.VMEM((240, 128), F32), in_specs=[a...]
    pallas_call x1, Pallas kernels: 1.55 us -> 0.66 us  [local(): pl.pallas_call(split, out_shape=(jax.ShapeDtypeStruct((48, 128), F32), ja...]
where the time goes in v4:
time: 74.2 us; the launch traced here: 74.1 us
  Pallas kernels  73.5 us (99%)
    pallas_call x1, Pallas kernels, local(): pl.pallas_call(kernel, out_shape=pltpu.VMEM((240, 128), F32), in_specs=[a...  72.8 us

profile of v4, /device:TPU:1, one launch (start us, length us, event | category | flops | bytes accessed | tf_op | source)
XLA Modules:
  0.0 74.1 jit_solution(12880529447800607002)
XLA Ops:
  0.6 72.8 %shard_map.95.both_ref = f32[240,128]{1,0:T(8,128)S(1)} custom-call(bf16[128,768]{1,0:T(8,128)(2,1)} %bitcast.15, f32[128,1536]{1,0:T(8,128)} %root_ref.1, bf16[768,1536]{1,0:T(8,128)(2,1)} %bitcast.11, bf16[1536,512]{1,0:T(8,128)(2,1)} %bitcast.13, bf16[1536,384]{1,0:T(8,128)(2,1)} %rinv_ref.1, bf16[192,4096]{1,0:T(8,128)(2,1)} %bitcast.14, ...), custom_call_target="tpu_custom_call" | custom-call | tf_op jit(solution)/shard_map/pallas_call | solution.py:389
  73.5 0.7 shard_map.96

commit v5 on v4

v5 whole, which is shorter than its diff:
```python
import jax
import jax.numpy as jnp
from jax import lax
from jax.experimental import pallas as pl
from jax.experimental.pallas import tpu as pltpu
from jax.sharding import PartitionSpec as P

BF = jnp.bfloat16
F32 = jnp.float32
MESH = pl.DeviceIdType.MESH
CONTRACT_LAST = (((1,), (1,)), ((), ()))

X_ORDER = (2, 1, 3)
NEAR = (0, 1, 7, 2, 6, 3, 5, 4)
GROUPS = ((0, 5), (5, 8))
SLOTS = 40
X_BLOCKS = X_ORDER + (0,)
Y_ORDER = (2, 1, 3)
Z_ORDER = (4, 3, 5, 2, 6, 1, 7)
Z_ARRIVAL = (4, 3, 5, 2, 6, 1, 7)
PLANE = sorted(
    ((dy, dx) for dy in range(4) for dx in range(4) if (dy, dx) != (0, 0)),
    key=lambda p: -(min(p[0], 4 - p[0]) + min(p[1], 4 - p[1])),
)
OWNERS = (
    (2, 2), (2, 1), (1, 2), (2, 3), (3, 2), (2, 0), (0, 2),
    (1, 1), (1, 3), (3, 1), (1, 0), (0, 1), (3, 3), (3, 0), (0, 3), (0, 0),
)
COL = [(dx, dh) for dx in (2, 1, 3) for dh in (1, 0)] + [(0, 1)]


def dot(a, b):
    return jnp.dot(a, b, preferred_element_type=F32)


def dot_last(a, b):
    return lax.dot_general(a, b, CONTRACT_LAST, preferred_element_type=F32)


def kernel(
    rhs_ref, root_ref, fwd_ref, coup_ref, rinv_ref, back_ref, bwd_ref, rows_ref,
    both_ref,
    rhs_v, fwd_v, coup_v, rinv_v, back_v, bwd_v, root_v, rows_v,
    part_f, part_b, core_in, x_f, x_out, x_in, rs_in, ag, y_keep,
    u_f, u_b, u_in, u_all, place, pick, p_rhs,
    xp_f, xp_b, xp_in, xr_all, rb_all, sel_out, sel_in, sel_all,
    z_out, a_f, b_f, a_in, b_in, a_out, b_out, fa_in, fb_in, own_f, own_in, flip, flip2,
    load_sem, send_sem, core_r, rs_r, xs_r, ag_r, pr_r, w_r, us_r, za_r, ya_r, xc_r, xo_r, rb_r, se_r, pl_r,
    a_r, b_r, fa_r, fb_r, end_r,
):
    l, r, q = lax.axis_index("leaf"), lax.axis_index("row"), lax.axis_index("col")
    x, h = q // 2, q % 2
    sib = (l, r, x * 2 + 1 - h)

    def xat(d):
        return lax.rem(x + d, 4)

    def yat(d):
        return lax.rem(r + d, 4)

    def zat(d):
        return lax.rem(l + d, 8)

    def load(src, dst, k):
        c = pltpu.make_async_copy(src, dst, load_sem.at[k])
        c.start()
        return c

    pending = []
    count = [0]

    def send(src, dst, rs, device):
        if len(pending) == SLOTS:
            pending.pop(0).wait_send()
        c = pltpu.make_async_remote_copy(
            src_ref=src, dst_ref=dst, send_sem=send_sem.at[count[0] % SLOTS], recv_sem=rs, device_id=device, device_id_type=MESH
        )
        c.start()
        count[0] += 1
        pending.append(c)

    def arrive(dst, rs):
        pltpu.make_async_remote_copy(
            src_ref=dst, dst_ref=dst, send_sem=send_sem.at[0], recv_sem=rs, device_id=sib, device_id_type=MESH
        ).wait_recv()

    def flush():
        while pending:
            pending.pop(0).wait_send()

    partners = [(l, r, xat(dx) * 2 + lax.rem(h + dh, 2)) for dx, dh in COL]
    partners += [(l, yat(dy), xat(dx) * 2 + h) for dy, dx in PLANE if dy]
    partners += [(l, yat(d), x * 2 + 1 - h) for d in Y_ORDER]
    partners += [(zat(d), r, q) for d in Z_ORDER[::-1]]
    bar = pltpu.get_barrier_semaphore()
    for p in partners[::-1]:
        pl.semaphore_signal(bar, inc=1, device_id=p, device_id_type=MESH)

    l_rhs = load(rhs_ref, rhs_v, 0)
    l_fwd = []
    for j, d in enumerate(X_BLOCKS):
        cols = pl.ds(pl.multiple_of(xat(d) * 384, 128), 384)
        l_fwd.append(load(fwd_ref.at[:, cols], fwd_v.at[j], 1 + j))
    l_coup = load(coup_ref, coup_v.at[h], 6)
    l_rows = load(rows_ref, rows_v.at[l], 5)

    l_rhs.wait()
    for j in range(4):
        l_fwd[j].wait()
        value = dot(rhs_v[...], fwd_v[j])
        part_f[j] = value
        part_b[j] = value.astype(BF)
        if j == 0:
            pl.semaphore_wait(bar, len(partners))
        for g in range(2):
            core = lax.rem(h + g, 2)
            if X_BLOCKS[j] or g:
                send(
                    part_b.at[j, pl.ds(pl.multiple_of(core * 64 + 32, 32), 32)], rs_in.at[min(2 * j + g, 6)], rs_r.at[0],
                    (l, r, xat(X_BLOCKS[j]) * 2 + core),
                )
        send(part_b.at[j, pl.ds(pl.multiple_of(64 - h * 64, 32), 32)], core_in.at[j], core_r.at[j], sib)
    l_root = [
        load(root_ref.at[pl.ds(pl.multiple_of(g * 64 + r * 16, 16), 16)], root_v.at[pl.ds(g * 16, 16)], 11 + g)
        for g in range(2)
    ]
    l_rinv = load(rinv_ref, rinv_v, 8)
    l_back = load(back_ref, back_v.at[h], 9)
    l_bwd = load(bwd_ref, bwd_v.at[h], 10)
    l_coup.wait()
    send(coup_v.at[h], coup_v.at[h], w_r.at[2], sib)
    for j, d in enumerate(X_BLOCKS):
        arrive(core_in.at[j], core_r.at[j])
        both = part_f[j, pl.ds(pl.multiple_of(h * 64, 32), 32), :] + core_in[j].astype(F32)
        x_f[j] = both
        x_out[j] = both.astype(BF)
        for i, e in enumerate(X_ORDER):
            block = xat(d)
            send(x_out.at[j], x_in.at[block, i], xs_r.at[block], (l, r, xat(e) * 2 + h))

    l_rows.wait()
    for j, d in enumerate(Z_ORDER):
        send(rows_ref, rows_v.at[l], pr_r.at[j], (zat(d), r, q))

    def build_place(leaf):
        row = rows_v[leaf, :, pl.ds(pl.multiple_of(q * 512, 512), 512)] - q * 1536

        @pl.loop(0, 12)
        def _(t):
            at = lax.broadcasted_iota(jnp.int32, (128, 512), 0) + t * 128
            place[leaf, pl.ds(pl.multiple_of(t * 128, 128), 128), :] = (at == row).astype(F32).astype(BF)

    def build_pick(leaf):
        row = rows_v[leaf, :, pl.ds(pl.multiple_of(l * 512 + r * 128, 128), 128)] - l * 1536

        @pl.loop(0, 12)
        def _(t):
            at = lax.broadcasted_iota(jnp.int32, (128, 128), 0) + t * 128
            pick[leaf, pl.ds(pl.multiple_of(t * 128, 128), 128), :] = (at == row).astype(F32).astype(BF)

    def rows_arrive(d):
        j = Z_ORDER.index((8 - d) % 8)
        arrive(rows_v.at[zat(d)], pr_r.at[j])

    build_place(l)

    total = part_f[3, pl.ds(pl.multiple_of(h * 64 + 32, 32), 32), :]
    arrive(rs_in, rs_r.at[0])
    for i in range(7):
        total = total + rs_in[i].astype(F32)
    y_keep[32:64, :] = total
    ag[x] = total.astype(BF)
    for i, e in enumerate(X_ORDER):
        send(ag.at[x], ag.at[x], ag_r.at[i], (l, r, xat(e) * 2 + h))
    for d in (1, 7, 2, 6):
        rows_arrive(d)
        build_place(zat(d))

    arrive(coup_v.at[1 - h], w_r.at[2])
    update = [jnp.zeros((64, 512), F32) for _ in range(2)]
    for d in (0, 1, 3, 2):
        block = xat(d)
        total = x_f[X_BLOCKS.index(d)]
        arrive(x_in.at[block], xs_r.at[block])
        for i in range(3):
            total = total + x_in[block, i].astype(F32)
        if d:
            i = X_ORDER.index((4 - d) % 4)
            arrive(ag.at[block], ag_r.at[i])
        else:
            y_keep[0:32, :] = total
        left = jnp.concatenate([total.astype(BF), ag[block]], axis=0)
        for g in range(2):
            update[g] = update[g] + dot(left, coup_v[g, pl.ds(pl.multiple_of(block * 384, 128), 384), :])

    for g in range(2):
        u_f[g] = update[g]
        u_b[g] = update[g].astype(BF)
    for g in (0, 1):
        core = lax.rem(h + g, 2)
        for i, d in enumerate(Y_ORDER + ((0,) if g else ())):
            k = pl.ds(pl.multiple_of(yat(d) * 16, 16), 16)
            send(
                u_b.at[core, k], u_in.at[g, i], us_r.at[g], (l, yat(d), x * 2 + core)
            )
    l_back.wait()
    l_bwd.wait()
    send(back_v.at[h], back_v.at[h], w_r.at[0], sib)
    send(bwd_v.at[h], bwd_v.at[h], w_r.at[1], sib)
    for d in (3, 5, 4):
        rows_arrive(d)
        build_place(zat(d))
    total = u_f[h, pl.ds(pl.multiple_of(r * 16, 16), 16), :]
    arrive(u_in.at[0, 0:3], us_r.at[0])
    for i in range(3):
        total = total + u_in[0, i].astype(F32)
    u_all[l, pl.ds(pl.multiple_of(h * 16, 16), 16), :] = total.astype(BF)
    total = jnp.zeros((16, 512), F32)
    arrive(u_in.at[1], us_r.at[1])
    for i in range(4):
        total = total + u_in[1, i].astype(F32)
    u_all[l, pl.ds(pl.multiple_of((1 - h) * 16, 16), 16), :] = total.astype(BF)

    for j, d in enumerate(Z_ORDER):
        send(u_all.at[l], u_all.at[l], za_r.at[j], (zat(d), r, q))
    for c in l_root:
        c.wait()
    placed = root_v[...] - dot_last(u_all[l], place[l])
    for d in Z_ARRIVAL[:6]:
        j = Z_ORDER.index((8 - d) % 8)
        leaf = zat(d)
        arrive(u_all.at[leaf], za_r.at[j])
        placed = placed - dot_last(u_all[leaf], place[leaf])
    d = Z_ARRIVAL[6]
    leaf = zat(d)
    arrive(u_all.at[leaf], za_r.at[Z_ORDER.index((8 - d) % 8)])

    for t in range(3):
        cols = slice(t * 512, t * 512 + 512)
        p_rhs[t, r] = (placed[:, cols] - dot_last(u_all[leaf], place[leaf, cols, :])).astype(BF)
        for i, d in enumerate(Y_ORDER):
            send(p_rhs.at[t, r], p_rhs.at[t, r], ya_r.at[t], (l, yat(d), q))
    for d in range(8):
        build_pick(zat(d))
    l_rinv.wait()
    value = jnp.zeros((128, 384), F32)
    for t in range(3):
        arrive(p_rhs.at[t, 0:3], ya_r.at[t])
        value = value + dot(p_rhs[t].reshape(128, 512), rinv_v[pl.ds(t * 512, 512), :])

    xp_f[...] = value
    xp_b[...] = value.astype(BF)
    for j, (dx, dh) in enumerate(COL):
        tx, th = xat(dx), lax.rem(h + dh, 2)
        k = pl.ds(pl.multiple_of(tx * 32 + th * 16, 16), 16)
        send(xp_b.at[k], xp_in.at[j], xc_r.at[0], (l, r, tx * 2 + th))
    own_k = pl.ds(pl.multiple_of(h * 64 + x * 16, 16), 16)
    total = xp_f[pl.ds(pl.multiple_of(x * 32 + h * 16, 16), 16), :]
    arrive(xp_in, xc_r.at[0])
    for j in range(7):
        total = total + xp_in[j].astype(F32)
    rb_all[r] = total.astype(BF)

    for d in Y_ORDER:
        send(rb_all.at[r], rb_all.at[r], rb_r.at[0], (l, yat(d), q))
    xr_all[own_k, :] = total
    for j, (dx, dh) in enumerate(COL):
        send(xr_all.at[own_k], xr_all.at[own_k], xo_r.at[0], (l, r, xat(dx) * 2 + lax.rem(h + dh, 2)))
    arrive(rb_all.at[0:3], rb_r.at[0])
    root_rows = jnp.concatenate([rb_all[t] for t in range(4)], axis=1)

    for d in Z_ORDER + (0,):
        child = zat(d)
        chosen = dot(root_rows, pick[child]).astype(BF)
        if d:
            n = NEAR.index(8 - d)
            sel_out[child] = chosen
            send(sel_out.at[child], sel_in.at[n], se_r.at[0 if n < GROUPS[0][1] else 1], (child, r, q))
        else:
            sel_in[0] = chosen
    arrive(xr_all.at[0:112], xo_r.at[0])
    flip[...] = xr_all[...].T
    both_ref[0:48, :] = flip[pl.ds(pl.multiple_of(q * 48, 16), 48), :]

    for g, (low, high) in enumerate(GROUPS):
        arrive(sel_in.at[max(low, 1) : high], se_r.at[g])
        for dy, dx in PLANE:
            send(
                sel_in.at[low:high], sel_all.at[r, x, low:high], pl_r.at[g, dy], (l, yat(dy), xat(dx) * 2 + h)
            )
        sel_all[r, x, low:high] = sel_in[low:high]
    arrive(back_v.at[1 - h], w_r.at[0])
    arrive(bwd_v.at[1 - h], w_r.at[1])
    corr = jnp.zeros((64, 384), F32)
    for g, (low, high) in enumerate(GROUPS):
        for dy in (0, 1, 3, 2):
            sr = yat(dy)
            arrive(sel_all.at[sr, 0 : 4 if dy else 3, low:high], pl_r.at[g, (4 - dy) % 4])
            left = jnp.concatenate([sel_all[sr, :, n].reshape(64, 128) for n in range(low, high)], axis=1)
            right = jnp.concatenate(
                [
                    back_v[:, :, pl.ds(pl.multiple_of(zat(NEAR[n]) * 512 + sr * 128, 128), 128)].reshape(384, 128)
                    for n in range(low, high)
                ],
                axis=1,
            )
            corr = corr + dot_last(left, right)
    reduced = (y_keep[...] - corr).astype(BF)

    for j, (dy, dx) in enumerate(OWNERS):
        cols = pl.ds(pl.multiple_of((yat(dy) * 4 + xat(dx)) * 384, 128), 384)
        value = dot(reduced, bwd_v[:, :, cols].reshape(384, 384))
        z_out[j] = value.astype(BF)
        if dx:
            send(z_out.at[j, 0:32], a_in.at[dy, dx - 1], a_r.at[dy], (l, r, xat(dx) * 2 + h))
        else:
            a_f[dy] = value[0:32]
        if dy:
            send(z_out.at[j, 32:64], b_in.at[dx, dy - 1], b_r.at[dx], (l, yat(dy), x * 2 + h))
        else:
            b_f[dx] = value[32:64]
    for c in pending[:-24]:
        c.wait_send()
    del pending[:-24]
    for d in (2, 1, 3, 0):
        for first, came, came_r, on, fin, fin_r, at in (
            (a_f, a_in, a_r, a_out, fa_in, fa_r, 0), (b_f, b_in, b_r, b_out, fb_in, fb_r, 32)
        ):
            total = first[d]
            arrive(came.at[d], came_r.at[d])
            for i in range(3):
                total = total + came[d, i].astype(F32)
            if d:
                on[d - 1] = total.astype(BF)
                for g in range(2):
                    to = (l, r, xat(d) * 2 + g) if at else (l, yat(d), x * 2 + g)
                    send(on.at[d - 1, :, g * 128 : g * 128 + 256], fin.at[d - 1, h], fin_r.at[d - 1], to)
            else:
                own_f[at : at + 32, :] = total

    send(
        own_f.at[:, pl.ds(pl.multiple_of((1 - h) * 128, 128), 256)], own_in.at[h], end_r.at[0], sib
    )
    own_in[h] = own_f[:, pl.ds(pl.multiple_of(h * 128, 128), 256)]
    flush()
    arrive(own_in.at[1 - h], end_r.at[0])
    for d in (2, 1, 3):
        for fin, fin_r, at in ((fa_in, fa_r, 0), (fb_in, fb_r, 32)):
            arrive(fin.at[d - 1], fin_r.at[d - 1])
            for c in range(2):
                own_in[c, at : at + 32] = own_in[c, at : at + 32] + fin[d - 1, c].astype(F32)
    flip2[...] = own_in[...].reshape(128, 256).T
    both_ref[48:240, :] = flip2[pl.ds(pl.multiple_of(h * 64, 64), 192), :]


def split(both_ref, xroot_ref, xchild_ref):
    xroot_ref[...] = both_ref[0:48, :]
    xchild_ref[...] = both_ref[48:240, :]


def local(
    rhs_child, rhs_root, fwd_child, coupling, root_inverse, back_child, bwd_child, parent_rows
):
    vm = pltpu.VMEM
    dma = pltpu.SemaphoreType.DMA
    scratch = [
        vm((128, 768), BF), vm((4, 768, 384), BF), vm((2, 1536, 512), BF), vm((1536, 384), BF),
        vm((2, 192, 4096), BF), vm((2, 192, 6144), BF), vm((32, 1536), F32), vm((8, 1, 4096), jnp.int32),
        vm((4, 128, 384), F32), vm((4, 128, 384), BF), vm((4, 32, 384), BF), vm((4, 32, 384), F32),
        vm((4, 32, 384), BF), vm((4, 3, 32, 384), BF), vm((7, 32, 384), BF), vm((4, 32, 384), BF), vm((64, 384), F32),
        vm((2, 64, 512), F32), vm((2, 64, 512), BF), vm((2, 4, 16, 512), BF), vm((8, 32, 512), BF),
        vm((8, 1536, 512), BF), vm((8, 1536, 128), BF), vm((3, 4, 32, 512), BF),
        vm((128, 384), F32), vm((128, 384), BF), vm((7, 16, 384), BF), vm((128, 384), F32),
        vm((4, 16, 384), BF), vm((8, 16, 128), BF), vm((8, 16, 128), BF), vm((4, 4, 8, 16, 128), BF),
        vm((16, 64, 384), BF), vm((4, 32, 384), F32), vm((4, 32, 384), F32),
        vm((4, 3, 32, 384), BF), vm((4, 3, 32, 384), BF), vm((3, 32, 384), BF), vm((3, 32, 384), BF),
        vm((3, 2, 32, 256), BF), vm((3, 2, 32, 256), BF), vm((64, 384), F32), vm((2, 64, 256), F32),
        vm((384, 128), F32), vm((256, 128), F32),
        dma((13,)), dma((SLOTS,)),
    ]
    for n in (4, 1, 4, 3, 7, 3, 2, 7, 3, 1, 1, 1, 2, (2, 4), 4, 4, 3, 3, 1):
        scratch.append(dma(n if isinstance(n, tuple) else (n,)))
    any_spec = pl.BlockSpec(memory_space=pl.ANY)
    vm_spec = pl.BlockSpec(memory_space=pltpu.VMEM)
    both = pl.pallas_call(
        kernel,
        out_shape=pltpu.VMEM((240, 128), F32),
        in_specs=[any_spec] * 8,
        out_specs=vm_spec,
        scratch_shapes=scratch,
        compiler_params=pltpu.CompilerParams(
            collective_id=0, has_side_effects=True, vmem_limit_bytes=56 * 2**20
        ),
    )(
        rhs_child[0], rhs_root, fwd_child[0], coupling[0], root_inverse, back_child[0].T, bwd_child[0], parent_rows
    )
    x_root, x_child = pl.pallas_call(
        split,
        out_shape=(jax.ShapeDtypeStruct((48, 128), F32), jax.ShapeDtypeStruct((192, 128), F32)),
        in_specs=[vm_spec],
        out_specs=(vm_spec, vm_spec),
    )(pltpu.with_memory_space_constraint(both, pltpu.VMEM))
    return (x_root.T, x_child.T[None])


def solution(mesh):
    placed = (
        P("leaf", None, "col"),
        P(None, "col"),
        P("leaf", "col", "row"),
        P("leaf", "row", "col"),
        P("col", ("leaf", "row")),
        P("leaf", None, ("row", "col")),
        P("leaf", ("row", "col"), None),
        P("leaf", None),
    )
    return jax.shard_map(
        local,
        mesh=mesh,
        in_specs=placed,
        out_specs=(P(None, ("leaf", "row", "col")), P("leaf", None, ("row", "col"))),
        check_vma=False,
    )
```

time: 74.2 us -> 71.6 us (0.965)
  Pallas kernels: 73.5 us -> 70.8 us
    pallas_call x1, Pallas kernels: 72.8 us -> 70.2 us  [local(): pl.pallas_call(kernel, out_shape=pltpu.VMEM((240, 128), F32), in_specs=[a...]
where the time goes in v5:
time: 71.6 us; the launch traced here: 71.5 us
  Pallas kernels  70.8 us (99%)
    pallas_call x1, Pallas kernels, local(): pl.pallas_call(kernel, out_shape=pltpu.VMEM((240, 128), F32), in_specs=[a...  70.2 us

profile of v5, /device:TPU:1, one launch (start us, length us, event | category | flops | bytes accessed | tf_op | source)
XLA Modules:
  0.0 71.5 jit_solution(13178753639707298026)
XLA Ops:
  0.6 70.2 %shard_map.95.both_ref = f32[240,128]{1,0:T(8,128)S(1)} custom-call(bf16[128,768]{1,0:T(8,128)(2,1)} %bitcast.15, f32[128,1536]{1,0:T(8,128)} %root_ref.1, bf16[768,1536]{1,0:T(8,128)(2,1)} %bitcast.11, bf16[1536,512]{1,0:T(8,128)(2,1)} %bitcast.13, bf16[1536,384]{1,0:T(8,128)(2,1)} %rinv_ref.1, bf16[192,4096]{1,0:T(8,128)(2,1)} %bitcast.14, ...), custom_call_target="tpu_custom_call" | custom-call | tf_op jit(solution)/shard_map/pallas_call | solution.py:385
  70.8 0.7 shard_map.96

commit v6 on v5

--- a/solution.py
+++ b/solution.py
@@ -13,7 +13,7 @@
 X_ORDER = (2, 1, 3)
 NEAR = (0, 1, 7, 2, 6, 3, 5, 4)
 GROUPS = ((0, 5), (5, 8))
-SLOTS = 40
+SLOTS = 24
 X_BLOCKS = X_ORDER + (0,)
 Y_ORDER = (2, 1, 3)
 Z_ORDER = (4, 3, 5, 2, 6, 1, 7)
@@ -46,7 +46,7 @@
     xp_f, xp_b, xp_in, xr_all, rb_all, sel_out, sel_in, sel_all,
     z_out, a_f, b_f, a_in, b_in, a_out, b_out, fa_in, fb_in, own_f, own_in, flip, flip2,
     load_sem, send_sem, core_r, rs_r, xs_r, ag_r, pr_r, w_r, us_r, za_r, ya_r, xc_r, xo_r, rb_r, se_r, pl_r,
-    a_r, b_r, fa_r, fb_r, end_r,
+    fa_r, fb_r, end_r,
 ):
     l, r, q = lax.axis_index("leaf"), lax.axis_index("row"), lax.axis_index("col")
     x, h = q // 2, q % 2
@@ -139,8 +139,8 @@
             send(x_out.at[j], x_in.at[block, i], xs_r.at[block], (l, r, xat(e) * 2 + h))
 
     l_rows.wait()
-    for j, d in enumerate(Z_ORDER):
-        send(rows_ref, rows_v.at[l], pr_r.at[j], (zat(d), r, q))
+    for d in Z_ORDER:
+        send(rows_ref, rows_v.at[l], pr_r.at[0 if d in (1, 7, 2, 6) else 1], (zat(d), r, q))
 
     def build_place(leaf):
         row = rows_v[leaf, :, pl.ds(pl.multiple_of(q * 512, 512), 512)] - q * 1536
@@ -157,10 +157,6 @@
         def _(t):
             at = lax.broadcasted_iota(jnp.int32, (128, 128), 0) + t * 128
             pick[leaf, pl.ds(pl.multiple_of(t * 128, 128), 128), :] = (at == row).astype(F32).astype(BF)
-
-    def rows_arrive(d):
-        j = Z_ORDER.index((8 - d) % 8)
-        arrive(rows_v.at[zat(d)], pr_r.at[j])
 
     build_place(l)
 
@@ -172,8 +168,8 @@
     ag[x] = total.astype(BF)
     for i, e in enumerate(X_ORDER):
         send(ag.at[x], ag.at[x], ag_r.at[i], (l, r, xat(e) * 2 + h))
+    arrive(rows_v.at[0:4], pr_r.at[0])
     for d in (1, 7, 2, 6):
-        rows_arrive(d)
         build_place(zat(d))
 
     arrive(coup_v.at[1 - h], w_r.at[2])
@@ -190,27 +186,25 @@
         else:
             y_keep[0:32, :] = total
         left = jnp.concatenate([total.astype(BF), ag[block]], axis=0)
+        rows = pl.ds(pl.multiple_of(block * 384, 128), 384)
         for g in range(2):
-            update[g] = update[g] + dot(left, coup_v[g, pl.ds(pl.multiple_of(block * 384, 128), 384), :])
-
-    for g in range(2):
-        u_f[g] = update[g]
-        u_b[g] = update[g].astype(BF)
-    for g in (0, 1):
-        core = lax.rem(h + g, 2)
-        for i, d in enumerate(Y_ORDER + ((0,) if g else ())):
-            k = pl.ds(pl.multiple_of(yat(d) * 16, 16), 16)
-            send(
-                u_b.at[core, k], u_in.at[g, i], us_r.at[g], (l, yat(d), x * 2 + core)
-            )
+            core = lax.rem(h + g, 2)
+            update[g] = update[g] + dot(left, coup_v[core, rows, :])
+            if d == 2:
+                u_b[g] = update[g].astype(BF)
+                for i, e in enumerate(Y_ORDER + ((0,) if g else ())):
+                    k = pl.ds(pl.multiple_of(yat(e) * 16, 16), 16)
+                    send(u_b.at[g, k], u_in.at[g, i], us_r.at[g], (l, yat(e), x * 2 + core))
+    u_f[...] = update[0]
+
     l_back.wait()
     l_bwd.wait()
     send(back_v.at[h], back_v.at[h], w_r.at[0], sib)
     send(bwd_v.at[h], bwd_v.at[h], w_r.at[1], sib)
+    arrive(rows_v.at[0:3], pr_r.at[1])
     for d in (3, 5, 4):
-        rows_arrive(d)
         build_place(zat(d))
-    total = u_f[h, pl.ds(pl.multiple_of(r * 16, 16), 16), :]
+    total = u_f[pl.ds(pl.multiple_of(r * 16, 16), 16), :]
     arrive(u_in.at[0, 0:3], us_r.at[0])
     for i in range(3):
         total = total + u_in[0, i].astype(F32)
@@ -312,11 +306,11 @@
         value = dot(reduced, bwd_v[:, :, cols].reshape(384, 384))
         z_out[j] = value.astype(BF)
         if dx:
-            send(z_out.at[j, 0:32], a_in.at[dy, dx - 1], a_r.at[dy], (l, r, xat(dx) * 2 + h))
+            send(z_out.at[j, 0:32], a_in.at[dy, dx - 1], core_r.at[dy], (l, r, xat(dx) * 2 + h))
         else:
             a_f[dy] = value[0:32]
         if dy:
-            send(z_out.at[j, 32:64], b_in.at[dx, dy - 1], b_r.at[dx], (l, yat(dy), x * 2 + h))
+            send(z_out.at[j, 32:64], b_in.at[dx, dy - 1], xs_r.at[dx], (l, yat(dy), x * 2 + h))
         else:
             b_f[dx] = value[32:64]
     for c in pending[:-24]:
@@ -324,7 +318,7 @@
     del pending[:-24]
     for d in (2, 1, 3, 0):
         for first, came, came_r, on, fin, fin_r, at in (
-            (a_f, a_in, a_r, a_out, fa_in, fa_r, 0), (b_f, b_in, b_r, b_out, fb_in, fb_r, 32)
+            (a_f, a_in, core_r, a_out, fa_in, fa_r, 0), (b_f, b_in, xs_r, b_out, fb_in, fb_r, 32)
         ):
             total = first[d]
             arrive(came.at[d], came_r.at[d])
@@ -368,7 +362,7 @@
         vm((2, 192, 4096), BF), vm((2, 192, 6144), BF), vm((32, 1536), F32), vm((8, 1, 4096), jnp.int32),
         vm((4, 128, 384), F32), vm((4, 128, 384), BF), vm((4, 32, 384), BF), vm((4, 32, 384), F32),
         vm((4, 32, 384), BF), vm((4, 3, 32, 384), BF), vm((7, 32, 384), BF), vm((4, 32, 384), BF), vm((64, 384), F32),
-        vm((2, 64, 512), F32), vm((2, 64, 512), BF), vm((2, 4, 16, 512), BF), vm((8, 32, 512), BF),
+        vm((64, 512), F32), vm((2, 64, 512), BF), vm((2, 4, 16, 512), BF), vm((8, 32, 512), BF),
         vm((8, 1536, 512), BF), vm((8, 1536, 128), BF), vm((3, 4, 32, 512), BF),
         vm((128, 384), F32), vm((128, 384), BF), vm((7, 16, 384), BF), vm((128, 384), F32),
         vm((4, 16, 384), BF), vm((8, 16, 128), BF), vm((8, 16, 128), BF), vm((4, 4, 8, 16, 128), BF),
@@ -378,7 +372,7 @@
         vm((384, 128), F32), vm((256, 128), F32),
         dma((13,)), dma((SLOTS,)),
     ]
-    for n in (4, 1, 4, 3, 7, 3, 2, 7, 3, 1, 1, 1, 2, (2, 4), 4, 4, 3, 3, 1):
+    for n in (4, 1, 4, 3, 2, 3, 2, 7, 3, 1, 1, 1, 2, (2, 4), 3, 3, 1):
         scratch.append(dma(n if isinstance(n, tuple) else (n,)))
     any_spec = pl.BlockSpec(memory_space=pl.ANY)
     vm_spec = pl.BlockSpec(memory_space=pltpu.VMEM)

time: 71.6 us -> 71.3 us (level)
  no operation moved by 1% of the time
where the time goes in v6:
time: 71.3 us; the launch traced here: 71.2 us
  Pallas kernels  70.6 us (99%)
    pallas_call x1, Pallas kernels, local(): pl.pallas_call(kernel, out_shape=pltpu.VMEM((240, 128), F32), in_specs=[a...  69.9 us

profile of v6, /device:TPU:1, one launch (start us, length us, event | category | flops | bytes accessed | tf_op | source)
XLA Modules:
  0.0 71.2 jit_solution(5294342155987975527)
XLA Ops:
  0.6 69.9 %shard_map.95.both_ref = f32[240,128]{1,0:T(8,128)S(1)} custom-call(bf16[128,768]{1,0:T(8,128)(2,1)} %bitcast.15, f32[128,1536]{1,0:T(8,128)} %root_ref.1, bf16[768,1536]{1,0:T(8,128)(2,1)} %bitcast.11, bf16[1536,512]{1,0:T(8,128)(2,1)} %bitcast.13, bf16[1536,384]{1,0:T(8,128)(2,1)} %rinv_ref.1, bf16[192,4096]{1,0:T(8,128)(2,1)} %bitcast.14, ...), custom_call_target="tpu_custom_call" | custom-call | tf_op jit(solution)/shard_map/pallas_call | solution.py:379
  70.5 0.7 shard_map.96

commit v7 on v6

--- a/solution.py
+++ b/solution.py
@@ -208,15 +208,19 @@
     arrive(u_in.at[0, 0:3], us_r.at[0])
     for i in range(3):
         total = total + u_in[0, i].astype(F32)
-    u_all[l, pl.ds(pl.multiple_of(h * 16, 16), 16), :] = total.astype(BF)
+    half = pl.ds(pl.multiple_of(h * 16, 16), 16)
+    u_all[l, half, :] = total.astype(BF)
+    for j, d in enumerate(Z_ORDER):
+        send(u_all.at[l, half], u_all.at[l, half], za_r.at[j], (zat(d), r, q))
     total = jnp.zeros((16, 512), F32)
     arrive(u_in.at[1], us_r.at[1])
     for i in range(4):
         total = total + u_in[1, i].astype(F32)
-    u_all[l, pl.ds(pl.multiple_of((1 - h) * 16, 16), 16), :] = total.astype(BF)
+    half = pl.ds(pl.multiple_of((1 - h) * 16, 16), 16)
+    u_all[l, half, :] = total.astype(BF)
 
     for j, d in enumerate(Z_ORDER):
-        send(u_all.at[l], u_all.at[l], za_r.at[j], (zat(d), r, q))
+        send(u_all.at[l, half], u_all.at[l, half], za_r.at[j], (zat(d), r, q))
     for c in l_root:
         c.wait()
     placed = root_v[...] - dot_last(u_all[l], place[l])

time: 71.3 us -> 71.1 us (level)
  no operation moved by 1% of the time
where the time goes in v7:
time: 71.1 us; the launch traced here: 71 us
  Pallas kernels  70.4 us (99%)
    pallas_call x1, Pallas kernels, local(): pl.pallas_call(kernel, out_shape=pltpu.VMEM((240, 128), F32), in_specs=[a...  69.7 us

profile of v7, /device:TPU:1, one launch (start us, length us, event | category | flops | bytes accessed | tf_op | source)
XLA Modules:
  0.0 71.0 jit_solution(13434717797893658106)
XLA Ops:
  0.6 69.7 %shard_map.95.both_ref = f32[240,128]{1,0:T(8,128)S(1)} custom-call(bf16[128,768]{1,0:T(8,128)(2,1)} %bitcast.15, f32[128,1536]{1,0:T(8,128)} %root_ref.1, bf16[768,1536]{1,0:T(8,128)(2,1)} %bitcast.11, bf16[1536,512]{1,0:T(8,128)(2,1)} %bitcast.13, bf16[1536,384]{1,0:T(8,128)(2,1)} %rinv_ref.1, bf16[192,4096]{1,0:T(8,128)(2,1)} %bitcast.14, ...), custom_call_target="tpu_custom_call" | custom-call | tf_op jit(solution)/shard_map/pallas_call | solution.py:383
  70.4 0.7 shard_map.96
